TPU v7x, 32 devices: a whole 2x2x4 slice. The times are simulated.
32 devices in a mesh: dom: 4 (over z), tile: 2 (over y), rep: 4 (over x, core).
Axes of the slice: x: 2, y: 2, z: 4, core: 2. Of those that a mesh axis runs over, the one named last changes fastest.
Arguments:
- quantizer_codes: int32 [8192, 32], P(('dom', 'tile', 'rep')), may hold values from 0 to 255
- codebook: bfloat16 [32, 256, 8], replicated, may hold values from -6 to 6
- adj_tiles: bfloat16 [32, 4, 256, 256], P(('dom', 'tile', 'rep')), may hold values from -0.3125 to 0.3125
- tile_list: int32 [32, 4, 2], P(('dom', 'tile', 'rep')), may hold values from 0 to 31, as said below
- tile_count: int32 [32], P(('dom', 'tile', 'rep')), may hold values from 1 to 4, as said below
- w_self: bfloat16 [256, 256], replicated, may hold values from -0.375 to 0.375
- w_neigh: bfloat16 [256, 256], replicated, may hold values from -0.375 to 0.375
- out_bias: float32 [256], replicated, may hold values from -3 to 3
- cotangent: bfloat16 [8192, 256], P(('dom', 'tile', 'rep')), may hold values from -0.625 to 0.625
Outputs:
- node_out: bfloat16 [8192, 256], P(('dom', 'tile', 'rep'))
- grad_self: float32 [256, 256], replicated
- grad_neigh: float32 [256, 256], replicated
- grad_bias: float32 [256], replicated
- grad_codebook: float32 [32, 256, 8], replicated
Inputs may be any that keep to these rules, and one draw needn't show every extreme that they name: `tile_list`: for device i (index along dom+tile+rep), every slot's row block r has r % 8 == i % 8 and its column block c has c // 8 == i // 8; slots at or beyond tile_count[i] are ignored. `tile_count`: some device has exactly 4 live slots.
All inputs are finite; a program needn't handle non-finite values.
Results may differ from a plain program's by a relative error of at most 0.0055.
Values may be sent and summed in bfloat16 or wider, within the bound.
A program may use at most 192 MiB of HBM per device.

v0:
```python
import jax
import jax.numpy as jnp
from jax import lax
from jax.sharding import PartitionSpec as P

HIGH = lax.Precision.HIGHEST
CONTRACT_ROWS = (((0,), (0,)), ((), ()))
CONTRACT_COLS = (((1,), (1,)), ((), ()))


def finish(pre_act):
    hidden = jax.nn.silu(pre_act)
    return hidden * lax.rsqrt(jnp.mean(hidden * hidden, axis=-1, keepdims=True) + 1e-05)


def one_hot_codes(code_rows, centroids):
    centroid_ids = jnp.arange(centroids, dtype=jnp.int32)
    return (code_rows[:, :, None] == centroid_ids[None, None, :]).astype(jnp.bfloat16)


def body(
    quantizer_codes,
    codebook,
    adj_tiles,
    tile_list,
    tile_count,
    w_self,
    w_neigh,
    out_bias,
    cotangent,
):
    group_size = lax.axis_size("tile") * lax.axis_size("rep")
    dom_count = lax.axis_size("dom")
    sub_count, centroids, sub_width = codebook.shape
    tile_side = adj_tiles.shape[2]
    slot_total = adj_tiles.shape[1]
    feat_width = sub_count * sub_width
    tile_data = adj_tiles[0]
    row_dom = tile_list[0, :, 0] // group_size
    col_pos = tile_list[0, :, 1] % group_size
    live_count = tile_count[0]
    live_mask = jnp.arange(slot_total, dtype=jnp.int32) < live_count
    own_onehot = one_hot_codes(quantizer_codes, centroids)
    feats = jnp.einsum("nmk,mke->nme", own_onehot, codebook, preferred_element_type=jnp.float32)
    feats = feats.reshape(tile_side, feat_width).astype(jnp.bfloat16)
    gathered = lax.all_gather(feats, ("tile", "rep"), axis=0, tiled=True).reshape(
        group_size, tile_side, feat_width
    )
    chosen = jnp.take(gathered, col_pos, axis=0)
    products = jnp.einsum("sij,sjf->sif", tile_data, chosen, preferred_element_type=jnp.float32)
    targets = jnp.arange(lax.axis_size("dom") * tile_side // tile_side, dtype=jnp.int32)
    select = ((row_dom[None, :] == targets[:, None]) & live_mask[None, :]).astype(jnp.float32)
    summed = jnp.einsum("ds,sif->dif", select, products, precision=HIGH)
    aggregate = lax.psum_scatter(
        summed.reshape(lax.axis_size("dom") * tile_side, feat_width),
        "dom",
        scatter_dimension=0,
        tiled=True,
    ).astype(jnp.bfloat16)
    pre_act = (
        jnp.dot(feats, w_self, preferred_element_type=jnp.float32)
        + jnp.dot(aggregate, w_neigh, preferred_element_type=jnp.float32)
        + out_bias
    )
    out_full, pullback = jax.vjp(finish, pre_act)
    node_out = out_full.astype(jnp.bfloat16)
    dpre = pullback(cotangent.astype(jnp.float32))[0].astype(jnp.bfloat16)
    grad_self = lax.dot_general(feats, dpre, CONTRACT_ROWS, preferred_element_type=jnp.float32)
    grad_neigh = lax.dot_general(aggregate, dpre, CONTRACT_ROWS, preferred_element_type=jnp.float32)
    grad_bias = jnp.sum(dpre.astype(jnp.float32), axis=0)
    dx_self = lax.dot_general(dpre, w_self, CONTRACT_COLS, preferred_element_type=jnp.float32)
    dagg = lax.dot_general(dpre, w_neigh, CONTRACT_COLS, preferred_element_type=jnp.float32).astype(
        jnp.bfloat16
    )
    dagg_all = lax.all_gather(dagg, "dom", axis=0, tiled=True).reshape(
        dom_count, tile_side, feat_width
    )
    picked = jnp.take(dagg_all, row_dom, axis=0)
    backprod = jnp.einsum("sij,sif->sjf", tile_data, picked, preferred_element_type=jnp.float32)
    column_ids = jnp.arange(group_size, dtype=jnp.int32)
    select_cols = ((col_pos[None, :] == column_ids[:, None]) & live_mask[None, :]).astype(
        jnp.float32
    )
    column = jnp.einsum("gs,sjf->gjf", select_cols, backprod, precision=HIGH)
    column_low = column.astype(jnp.bfloat16)
    sub_dx = dx_self.reshape(tile_side, sub_count, sub_width)
    received = lax.all_to_all(column_low, ("tile", "rep"), split_axis=0, concat_axis=0, tiled=True)
    input_gradient_total = sub_dx + jnp.sum(received.astype(jnp.float32), axis=0).reshape(
        tile_side, sub_count, sub_width
    )
    grad_codebook = jnp.einsum(
        "nmk,nme->mke",
        own_onehot,
        input_gradient_total,
        precision=HIGH,
        preferred_element_type=jnp.float32,
    )
    grad_self, grad_neigh, grad_bias, grad_codebook = lax.psum(
        (grad_self, grad_neigh, grad_bias, grad_codebook), ("dom", "tile", "rep")
    )
    return (node_out, grad_self, grad_neigh, grad_bias, grad_codebook)


def solution(mesh):
    in_specs = (
        P(("dom", "tile", "rep"), None),
        P(),
        P(("dom", "tile", "rep"), None, None, None),
        P(("dom", "tile", "rep"), None, None),
        P(("dom", "tile", "rep")),
        P(),
        P(),
        P(),
        P(("dom", "tile", "rep"), None),
    )
    out_specs = (P(("dom", "tile", "rep"), None), P(), P(), P(), P())
    return jax.shard_map(body, mesh=mesh, in_specs=in_specs, out_specs=out_specs, check_vma=False)
```

profile of v0, /device:TPU:0, one launch (start us, length us, event | category | flops | bytes accessed | tf_op | source)
XLA Modules:
  0.0 252.3 jit_solution(17830671682866264838)
XLA Ops:
  7.2 0.0 copy-start
  7.2 0.0 copy-start.7
  7.2 0.0 all-gather.2.cloned.1.call-start
  7.2 3.2 %fusion.7 = bf16[256,256]{0,1:T(8,128)(2,1)} fusion(bf16[32,256,8]{1,2,0:T(8,128)(2,1)} %param.10, s32[256,32]{0,1:T(8,128)} %param.9), kind=kOutput, calls=%fused_computation.17 | convolution fusion | flops 35717120 | bytes 294912 | tf_op jit(solution)/shard_map/nmk,mke->nme/dot_general | solution.py:44
  10.4 0.0 all-gather.2.cloned.1.call-update
  10.5 0.0 reduce-scatter.2.cloned.1.call-start
  11.2 25.7 %all-gather.2.cloned.1.call-done = bf16[2048,256]{0,1:T(8,128)(2,1)} async-done(((bf16[256,256]{0,1:T(8,128)(2,1)}), bf16[2048,256]{0,1:T(8,128)(2,1)}) %all-gather.2.cloned.1.call-update) | async-done | bytes 1048592 | tf_op jit(solution)/shard_map/all_gather | solution.py:46
  36.9 1.5 copy.20
  38.4 0.6 gather_fusion
  39.0 0.0 copy-done
  39.0 0.4 convolution_bitcast_fusion.1
  39.4 0.4 copy.22
  39.8 1.1 fusion.26
  40.9 1.2 copy.23
  42.1 0.0 copy-start.9
  42.1 0.0 reduce-scatter.2.cloned.1.call-update
  42.1 0.9 copy-done.6
  42.9 0.1 copy.24
  43.1 0.2 fusion.43
  43.3 26.1 %reduce-scatter.2.cloned.1.call-done = f32[256,256]{1,0:T(8,128)} async-done(((f32[1024,256]{1,0:T(8,128)}), f32[256,256]{1,0:T(8,128)}) %reduce-scatter.2.cloned.1.call-update) | async-done | bytes 262160 | tf_op jit(solution)/shard_map/reduce_scatter | solution.py:54
  69.4 0.0 copy-done.9
  69.4 1.3 fusion.14
  70.7 0.3 convert_reduce_fusion.1
  70.9 0.2 convolution_convert_fusion.1
  71.2 16.0 %all_gather.7 = bf16[1024,256]{1,0:T(8,128)(2,1)S(1)} all-gather(bf16[256,256]{1,0:T(8,128)(2,1)S(1)} %convolution_convert_fusion.1), channel_id=1, replica_groups=mesh['dom'=4,'tile'=2,'rep'=4] {'dom'}, dimensions={0}, use_global_device_ids=true | all-gather | bytes 655360 | tf_op jit(solution)/shard_map/all_gather | solution.py:75
  87.2 0.6 gather_fusion.1
  87.8 0.4 convolution_bitcast_fusion
  88.2 0.4 copy.26
  88.6 1.4 convolution_convert_fusion
  90.0 1.2 copy.27
  91.2 3.8 %all-to-all-start = ((bf16[8,256,256]{2,1,0:T(8,128)(2,1)}), bf16[8,256,256]{2,1,0:T(8,128)(2,1)S(1)}, u32[]{:S(2)}, u32[]{:S(2)}) async-start(bf16[8,256,256]{2,1,0:T(8,128)(2,1)} %copy.27), calls=%async_computation.1 | async-start | bytes 2097152 | tf_op jit(solution)/shard_map/all_to_all | solution.py:87
  94.9 0.0 all-reduce.3.cloned.1.call-start
  95.0 0.9 fusion.44
  95.9 0.0 copy-done.3
  95.9 0.9 fusion.21
  96.8 13.5 %all-to-all-done = bf16[8,256,256]{2,1,0:T(8,128)(2,1)S(1)} async-done(((bf16[8,256,256]{2,1,0:T(8,128)(2,1)}), bf16[8,256,256]{2,1,0:T(8,128)(2,1)S(1)}, u32[]{:S(2)}, u32[]{:S(2)}) %all-to-all-start) | async-done | bytes 1048608 | tf_op jit(solution)/shard_map/all_to_all | solution.py:87
  110.3 0.1 convert_reduce_fusion
  110.5 0.1 copy.29
  110.6 0.2 fusion.4
  110.8 3.8 %fusion = f32[32,256,8]{1,2,0:T(8,128)} fusion(f32[256,32,8]{0,2,1:T(8,128)S(1)} %fusion.4, s32[256,32]{0,1:T(8,128)S(1)} %copy-done.8), kind=kOutput, calls=%fused_computation.3 | convolution fusion | flops 203423744 | bytes 557056 | tf_op jit(solution)/shard_map/nmk,nme->mke/dot_general | solution.py:91
  114.7 0.0 all-reduce.3.cloned.1.call-update
  114.7 0.8 copy.30
  115.5 37.7 %psum.30 = f32[256]{0:T(256)} all-reduce(f32[256]{0:T(256)S(1)} %get-tuple-element.25), channel_id=1, replica_groups=mesh['dom'=4,'tile'=2,'rep'=4] {'dom','tile','rep'}, use_global_device_ids=true, to_apply=%region_6.7 | all-reduce | flops 256 | bytes 2048 | tf_op jit(solution)/shard_map/psum | solution.py:98
  153.2 88.5 %all-reduce.3.cloned.1.call-done = (f32[256,256]{1,0:T(8,128)}, f32[256,256]{1,0:T(8,128)}, f32[32,256,8]{1,2,0:T(8,128)}) async-done(((f32[256,256]{1,0:T(8,128)}, f32[256,256]{1,0:T(8,128)}, f32[32,256,8]{1,2,0:T(8,128)}), (f32[256,256]{1,0:T(8,128)}, f32[256,256]{1,0:T(8,128)}, f32[32,256,8]{1,2,0:T(8,128)})) %all-reduce.3.cloned.1.call-update) | async-done | bytes 786448 | tf_op jit(solution)/shard_map/psum | solution.py:98
  241.7 1.7 copy.38
  243.4 1.7 copy.39
  245.1 0.0 copy-done.4
  245.1 0.7 copy.40
  (17 shorter events, 0.1 us)
Async XLA Ops:
  7.2 31.8 %copy-start = (bf16[1,4,256,256]{3,2,1,0:T(8,128)(2,1)S(1)}, bf16[1,4,256,256]{3,2,1,0:T(8,128)(2,1)}, u32[]{:S(2)}) copy-start(bf16[1,4,256,256]{3,2,1,0:T(8,128)(2,1)} %param.11) | copy-start | bytes 1572868
  7.2 4.0 %copy-start.7 = (s32[1,4,2]{1,2,0:T(2,128)S(1)}, s32[1,4,2]{1,2,0:T(2,128)}, u32[]{:S(2)}) copy-start(s32[1,4,2]{1,2,0:T(2,128)} %param.12) | copy-start | bytes 100
  7.2 29.7 %all-gather.2.cloned.1.call-start = ((), (), s32[]{:S(2)}) async-start(), calls=%async_computation.2 | async-start | bytes 1179648 | tf_op jit(solution)/shard_map/all_gather | solution.py:46
  10.5 58.9 %reduce-scatter.2.cloned.1.call-start = ((), (), s32[]{:S(2)}) async-start(), calls=%async_computation.3 | async-start | bytes 1310720 | tf_op jit(solution)/shard_map/reduce_scatter | solution.py:54
  42.0 0.9 copy-start.6
  42.0 1.0 copy-start.1
  42.0 1.0 copy-start.2
  42.1 27.3 %copy-start.5 = (bf16[256,256]{1,0:T(8,128)(2,1)S(1)}, bf16[256,256]{1,0:T(8,128)(2,1)}, u32[]{:S(2)}) copy-start(bf16[256,256]{1,0:T(8,128)(2,1)} %param.15) | copy-start | bytes 393220
  42.1 27.3 %copy-start.9 = (f32[256]{0:T(256)S(1)}, f32[256]{0:T(256)}, u32[]{:S(2)}) copy-start(f32[256]{0:T(256)} %param.16) | copy-start | bytes 3076
  91.2 4.7 %copy-start.3 = (f32[256,256]{1,0:T(8,128)S(1)}, f32[256,256]{1,0:T(8,128)}, u32[]{:S(2)}) copy-start(f32[256,256]{1,0:T(8,128)} %reduce-scatter.2.cloned.1.call-done) | copy-start | bytes 786436
  91.2 19.2 %all-to-all-start = ((bf16[8,256,256]{2,1,0:T(8,128)(2,1)}), bf16[8,256,256]{2,1,0:T(8,128)(2,1)S(1)}, u32[]{:S(2)}, u32[]{:S(2)}) async-start(bf16[8,256,256]{2,1,0:T(8,128)(2,1)} %copy.27), calls=%async_computation.1 | async-start | bytes 2097152 | tf_op jit(solution)/shard_map/all_to_all | solution.py:87
  94.9 146.8 %all-reduce.3.cloned.1.call-start = ((), (), s32[]{:S(2)}) async-start(), calls=%async_computation.4 | async-start | bytes 1572864 | tf_op jit(solution)/shard_map/psum | solution.py:98
  96.8 14.0 %copy-start.8 = (s32[256,32]{0,1:T(8,128)S(1)}, s32[256,32]{0,1:T(8,128)}, u32[]{:S(2)}) copy-start(s32[256,32]{0,1:T(8,128)} %param.9) | copy-start | bytes 98308
  241.7 3.4 %copy-start.4 = (f32[32,256,8]{1,2,0:T(8,128)S(1)}, f32[32,256,8]{1,2,0:T(8,128)}, u32[]{:S(2)}) copy-start(f32[32,256,8]{1,2,0:T(8,128)} %get-tuple-element.44) | copy-start | bytes 786436
Sparse Core Ops, SparseCore 0:
  10.6 26.2 all-gather.1
  42.2 27.1 reduce-scatter.1
  114.8 126.8 all-reduce.2
where the time goes:
time: 253 us; the launch traced here: 252 us
  waiting for transfers between devices  154 us (61%)
  blocking collectives  53.8 us (21%)
  between operations  14.6 us (6%)
  matrix products  14.1 us (6%)
  local copies, waits for them, and re-layouts  11.7 us (5%)
  starting transfers between devices  3.89 us (2%)
    psum x1, waiting for transfers between devices, body(): lax.psum((grad_self, grad_neigh, grad_bias, grad_codebook), ('dom', 'tile...  88.5 us
    psum x1, blocking collectives, body(): lax.psum((grad_self, grad_neigh, grad_bias, grad_codebook), ('dom', 'tile...  37.7 us
    reduce_scatter x1, waiting for transfers between devices, body(): lax.psum_scatter(summed.reshape(lax.axis_size('dom') * tile_side, feat_wi...  26.1 us
    all_gather x1, waiting for transfers between devices, body(): lax.all_gather(feats, ('tile', 'rep'), axis=0, tiled=True)  25.7 us
    all_gather x1, blocking collectives, body(): lax.all_gather(dagg, 'dom', axis=0, tiled=True)  16 us
    all_to_all x1, waiting for transfers between devices, body(): lax.all_to_all(column_low, ('tile', 'rep'), split_axis=0, concat_axis=0,...  13.5 us
    unnamed x25, local copies, waits for them, and re-layouts  5.84 us
  transfers between devices with their start and end apart: 4, of which 4 were waited for; matrix products, arithmetic and copies ran while one was open for 1% of the time, Pallas kernels for 0%

commit v1 on v0

v1 whole, which is shorter than its diff:
```python
import functools

import jax
import jax.numpy as jnp
from jax import lax
from jax.experimental import pallas as pl
from jax.experimental.pallas import tpu as pltpu
from jax.sharding import PartitionSpec as P

F32, BF16 = jnp.float32, jnp.bfloat16
MESH = pl.DeviceIdType.MESH
NN = (((1,), (0,)), ((), ()))
NT = (((1,), (1,)), ((), ()))
CHUNKS = 2
ROWS16 = 16


def mm(a, b, dims=NN):
    return lax.dot_general(a, b, dims, preferred_element_type=F32)


def each(low, high, fn):
    if high - low <= 8:
        for k in range(low, high):
            fn(k)
    else:
        lax.fori_loop(low, high, lambda k, c: (fn(k), c)[1], 0)


def kernel(cfg, *refs):
    doms, tiles, reps, slots, side, feat, subs, cents, reduce_here = cfg
    group = tiles * reps
    width = feat // subs
    part = side // CHUNKS
    (codes_ref, book_ref, adj_ref, list_ref, count_ref, ws_ref, wn_ref, bias_ref, cot_ref) = refs[:9]
    out_ref, gsn_ref, gb_ref, gc_ref = refs[9:13]
    (codes_all, codes_one, onehot, feats_t, slot_t, feats, self_act, part_own, part_send, part_recv,
     agg, dpre, dagg_0, dagg_1, back, dx, col_send, col_recv,
     codes_s, codes_r, part_s, part_r, dagg_s, dagg_r, col_s, col_r) = refs[13:39]

    dagg_all = (dagg_0, dagg_1)
    d = lax.axis_index("dom")
    g = lax.axis_index("tile") * reps + lax.axis_index("rep")

    def group_peer(k):
        p = lax.rem(g + k, group)
        return p, {"tile": lax.div(p, reps), "rep": lax.rem(p, reps)}

    def group_source(k):
        return lax.rem(g + group - k, group)

    def dom_peer(k):
        p = lax.rem(d + k, doms)
        return p, {"dom": p}

    def dom_source(k):
        return lax.rem(d + doms - k, doms)

    def copy(src, dst, send, recv, device):
        return pltpu.make_async_remote_copy(
            src_ref=src, dst_ref=dst, send_sem=send, recv_sem=recv, device_id=device, device_id_type=MESH
        )

    barrier = pltpu.get_barrier_semaphore()
    each(1, group, lambda k: pl.semaphore_signal(barrier, inc=1, device_id=group_peer(k)[1], device_id_type=MESH))
    each(1, doms, lambda k: pl.semaphore_signal(barrier, inc=1, device_id=dom_peer(k)[1], device_id_type=MESH))
    codes_all[g] = codes_ref[...].astype(F32).astype(BF16)
    codes_one[...] = codes_ref[...].astype(F32)
    pl.semaphore_wait(barrier, group + doms - 2)

    def codes_copy(k):
        return copy(codes_all.at[g], codes_all.at[g], codes_s.at[k], codes_r.at[k], group_peer(k)[1])

    def codes_wait(k):
        src = group_source(k)
        copy(codes_all.at[src], codes_all.at[src], codes_s.at[k], codes_r.at[k], group_peer(k)[1]).wait_recv()

    each(1, group, lambda k: codes_copy(k).start())

    cent_ids = lax.broadcasted_iota(jnp.int32, (cents, side), 0).astype(F32)

    def decode(dst, keep):
        def step(it, carry):
            slab = codes_one[pl.ds(pl.multiple_of(it * 8, 8), 8), :]
            for pair in range(4):
                rows = pl.ds(pl.multiple_of(it * (8 * width) + pair * 2 * width, 16), 2 * width)
                lhs = book_ref[rows, :]
                halves = []
                for odd in range(2):
                    at = pair * 2 + odd
                    hot = jnp.where(slab[at:at + 1, :] == cent_ids, 1.0, 0.0).astype(BF16)
                    if keep:
                        onehot[it * 8 + at] = hot
                    halves.append(mm(lhs, hot)[odd * width:(odd + 1) * width, :])
                dst[rows, :] = jnp.concatenate(halves, axis=0).astype(BF16)
            return carry
        lax.fori_loop(0, subs // 8, step, 0)

    decode(feats_t, True)
    feats[...] = feats_t[...].astype(F32).T.astype(BF16)
    self_act[...] = mm(feats[...], ws_ref[...]) + bias_ref[...]

    live = [jnp.where(s < count_ref[0], 1.0, 0.0).astype(F32) for s in range(slots)]
    row_dom = [lax.div(list_ref[s, 0], group) for s in range(slots)]
    col_pos = [lax.rem(list_ref[s, 1], group) for s in range(slots)]

    each(1, group, codes_wait)
    for s in range(slots):
        codes_one[...] = codes_all[col_pos[s]].astype(F32)
        decode(slot_t.at[s], False)

    def part_copy(c, k):
        return copy(part_send.at[c, k], part_recv.at[c, k], part_s.at[c, k], part_r.at[c, k], dom_peer(k)[1])

    for c in range(CHUNKS):
        rows = slice(c * part, (c + 1) * part)
        prods = [mm(adj_ref[s, rows, :], slot_t[s], NT) * live[s] for s in range(slots)]
        for k in list(range(1, doms)) + [0]:
            to = dom_peer(k)[0]
            total = sum(prods[s] * jnp.where(row_dom[s] == to, 1.0, 0.0).astype(F32) for s in range(slots))
            if k:
                part_send[c, k] = total.astype(BF16)
                part_copy(c, k).start()
            else:
                part_own[rows, :] = total

    def dagg_copy(c, k):
        return copy(dagg_all[c].at[d], dagg_all[c].at[d], dagg_s.at[c, k], dagg_r.at[c, k], dom_peer(k)[1])

    def dagg_wait(c, k):
        src = dom_source(k)
        copy(dagg_all[c].at[src], dagg_all[c].at[src], dagg_s.at[c, k], dagg_r.at[c, k], dom_peer(k)[1]).wait_recv()

    for c in range(CHUNKS):
        rows = slice(c * part, (c + 1) * part)
        total = part_own[rows, :]
        for k in range(1, doms):
            part_copy(c, k).wait_recv()
            total = total + part_recv[c, k].astype(F32)
        low = total.astype(BF16)
        agg[rows, :] = low
        pre = self_act[rows, :] + mm(low, wn_ref[...])
        sig = 1.0 / (1.0 + jnp.exp(-pre))
        hidden = pre * sig
        scale = lax.rsqrt(jnp.mean(hidden * hidden, axis=-1, keepdims=True) + 1e-05)
        out_ref[rows, :] = (hidden * scale).astype(BF16)
        cot = cot_ref[rows, :].astype(F32)
        along = jnp.mean(cot * hidden, axis=-1, keepdims=True)
        dhid = scale * cot - hidden * (scale * scale * scale * along)
        grad = (dhid * (sig * (1.0 + pre * (1.0 - sig)))).astype(BF16)
        dpre[rows, :] = grad
        dagg_all[c][d] = mm(wn_ref[...], grad, NT).astype(BF16)
        for k in range(1, doms):
            dagg_copy(c, k).start()

    dpre_all = dpre[...]
    grad_self = mm(feats_t[...], dpre_all)
    grad_neigh = mm(agg[...].astype(F32).T.astype(BF16), dpre_all)
    grad_bias = jnp.sum(dpre_all.astype(F32).reshape(side // 8, 8, feat), axis=0)

    if reduce_here:
        (gs, g_recv, g_mid, gz_recv, g_fin, cs, c_recv, c_mid, cz_recv, c_fin, b_grp, b_dom,
         g1s, g1r, g2s, g2r, g3s, g3r, g4s, g4r, c1s, c1r, c2s, c2r, c3s, c3r, c4s, c4r,
         b1s, b1r, b2s, b2r) = refs[39:]

        def rs_group(src, dst, ss, rr):
            def go(k):
                p, device = group_peer(k)
                return copy(src.at[p], dst.at[k], ss.at[k], rr.at[k], device)
            return go

        def rs_dom(src, dst, ss, rr):
            def go(k):
                p, device = dom_peer(k)
                return copy(src.at[p], dst.at[k], ss.at[k], rr.at[k], device)
            return go

        def ag_dom(own, slot, ss, rr):
            def go(k):
                return copy(own, own, ss.at[k], rr.at[k], dom_peer(k)[1])

            def wait(k):
                at = slot(dom_source(k))
                copy(at, at, ss.at[k], rr.at[k], dom_peer(k)[1]).wait_recv()
            return go, wait

        def ag_group(buf, ss, rr):
            def go(k):
                return copy(buf.at[g], buf.at[g], ss.at[k], rr.at[k], group_peer(k)[1])

            def wait(k):
                at = buf.at[group_source(k)]
                copy(at, at, ss.at[k], rr.at[k], group_peer(k)[1]).wait_recv()
            return go, wait

        sends = []

        def start(go, n):
            for k in range(1, n):
                go(k).start()
            sends.append((go, n))

        g1 = rs_group(gs, g_recv, g1s, g1r)
        g2 = rs_dom(g_mid, gz_recv, g2s, g2r)
        g3 = ag_dom(g_fin.at[g, d], lambda at: g_fin.at[g, at], g3s, g3r)
        g4 = ag_group(g_fin, g4s, g4r)
        c1 = rs_group(cs, c_recv, c1s, c1r)
        c2 = rs_dom(c_mid, cz_recv, c2s, c2r)
        c3 = ag_dom(c_fin.at[g, d], lambda at: c_fin.at[g, at], c3s, c3r)
        c4 = ag_group(c_fin, c4s, c4r)
        b1 = ag_group(b_grp, b1s, b1r)
        b2 = ag_dom(b_dom.at[d], lambda at: b_dom.at[at], b2s, b2r)

        half = group // 2
        gs[0:half] = grad_self.astype(BF16).reshape(half, doms, ROWS16, feat)
        gs[half:group] = grad_neigh.astype(BF16).reshape(half, doms, ROWS16, feat)
        b_grp[g] = grad_bias
        start(g1, group)
        start(b1[0], group)
    else:
        gsn_ref[0:feat, :] = grad_self
        gsn_ref[feat:2 * feat, :] = grad_neigh
        gb_ref[...] = grad_bias

    dx[...] = mm(ws_ref[...], dpre_all, NT)

    for c in range(CHUNKS):
        for k in range(1, doms):
            dagg_wait(c, k)
        for s in range(slots):
            prod = mm(dagg_all[c][row_dom[s]], adj_ref[s, c * part:(c + 1) * part, :]) * live[s]
            back[s] = prod if c == 0 else back[s] + prod

    def col_copy(k):
        return copy(col_send.at[k], col_recv.at[k], col_s.at[k], col_r.at[k], group_peer(k)[1])

    def column(k):
        to = group_peer(k)[0]
        return sum(back[s] * jnp.where(col_pos[s] == to, 1.0, 0.0).astype(F32) for s in range(slots))

    def send_column(k):
        col_send[k] = column(k).astype(BF16)
        col_copy(k).start()

    each(1, group, send_column)
    dx[...] = dx[...] + column(0)

    if reduce_here:
        mid = gs[g].astype(F32)
        for k in range(1, group):
            g1(k).wait_recv()
            mid = mid + g_recv[k].astype(F32)
        g_mid[...] = mid.astype(BF16)
        start(g2, doms)
        for k in range(1, group):
            b1[1](k)
        b_dom[d] = jnp.sum(b_grp[...], axis=0)
        start(b2[0], doms)
        fin = g_mid[d].astype(F32)
        for k in range(1, doms):
            g2(k).wait_recv()
            fin = fin + gz_recv[k].astype(F32)
        g_fin[g, d] = fin.astype(BF16)
        start(g3[0], doms)
        for k in range(1, doms):
            g3[1](k)
        start(g4[0], group)

    def add_column(k):
        col_copy(k).wait_recv()
        dx[...] = dx[...] + col_recv[k].astype(F32)

    each(1, group, add_column)

    def code_step(it, carry):
        for at in range(8):
            rows = pl.ds(pl.multiple_of(it * (8 * width) + at * width, 8), width)
            full = dx[rows, :]
            high = full.astype(BF16).astype(F32)
            both = jnp.concatenate([high, full - high], axis=0).astype(BF16)
            two = mm(both, onehot[it * 8 + at], NT)
            gc_ref[rows, :] = two[0:width, :] + two[width:2 * width, :]
        return carry

    lax.fori_loop(0, subs // 8, code_step, 0)

    if reduce_here:
        lanes = cents // 2
        for h in range(2):
            cs[h * half:(h + 1) * half] = (
                gc_ref[:, h * lanes:(h + 1) * lanes].astype(BF16).reshape(half, doms, ROWS16, lanes)
            )
        start(c1, group)
        for k in range(1, group):
            g4[1](k)
        gsn_ref[...] = g_fin[...].astype(F32).reshape(2 * feat, feat)
        for k in range(1, doms):
            b2[1](k)
        gb_ref[...] = jnp.broadcast_to(jnp.sum(jnp.sum(b_dom[...], axis=0), axis=0, keepdims=True), (8, feat))
        mid = cs[g].astype(F32)
        for k in range(1, group):
            c1(k).wait_recv()
            mid = mid + c_recv[k].astype(F32)
        c_mid[...] = mid.astype(BF16)
        start(c2, doms)
        fin = c_mid[d].astype(F32)
        for k in range(1, doms):
            c2(k).wait_recv()
            fin = fin + cz_recv[k].astype(F32)
        c_fin[g, d] = fin.astype(BF16)
        start(c3[0], doms)
        for k in range(1, doms):
            c3[1](k)
        start(c4[0], group)
        for k in range(1, group):
            c4[1](k)
        for h in range(2):
            gc_ref[:, h * lanes:(h + 1) * lanes] = (
                c_fin[h * half:(h + 1) * half].astype(F32).reshape(feat, lanes)
            )
        for go, n in sends:
            for k in range(1, n):
                go(k).wait_send()

    each(1, group, lambda k: codes_copy(k).wait_send())
    each(1, group, lambda k: col_copy(k).wait_send())
    for c in range(CHUNKS):
        for k in range(1, doms):
            part_copy(c, k).wait_send()
            dagg_copy(c, k).wait_send()


def body(quantizer_codes, codebook, adj_tiles, tile_list, tile_count, w_self, w_neigh, out_bias, cotangent):
    doms, tiles, reps = (lax.axis_size(a) for a in ("dom", "tile", "rep"))
    group = tiles * reps
    subs, cents, width = codebook.shape
    feat = subs * width
    slots, side = adj_tiles.shape[1], adj_tiles.shape[2]
    part = side // CHUNKS
    reduce_here = group % 2 == 0 and group * doms * ROWS16 == 2 * feat and feat == cents
    cfg = (doms, tiles, reps, slots, side, feat, subs, cents, reduce_here)
    vm, dma = pltpu.VMEM, pltpu.SemaphoreType.DMA
    scratch = [
        vm((group, subs, side), BF16), vm((subs, side), F32), vm((subs, cents, side), BF16),
        vm((feat, side), BF16), vm((slots, feat, side), BF16), vm((side, feat), BF16), vm((side, feat), F32),
        vm((side, feat), F32), vm((CHUNKS, doms, part, feat), BF16), vm((CHUNKS, doms, part, feat), BF16),
        vm((side, feat), BF16), vm((side, feat), BF16), vm((doms, feat, part), BF16), vm((doms, feat, part), BF16),
        vm((slots, feat, side), F32), vm((feat, side), F32),
        vm((group, feat, side), BF16), vm((group, feat, side), BF16),
        dma((group,)), dma((group,)), dma((CHUNKS, doms)), dma((CHUNKS, doms)),
        dma((CHUNKS, doms)), dma((CHUNKS, doms)), dma((group,)), dma((group,)),
    ]
    if reduce_here:
        for lanes in (feat, cents // 2):
            scratch += [
                vm((group, doms, ROWS16, lanes), BF16), vm((group, doms, ROWS16, lanes), BF16),
                vm((doms, ROWS16, lanes), BF16), vm((doms, ROWS16, lanes), BF16),
                vm((group, doms, ROWS16, lanes), BF16),
            ]
        scratch += [vm((group, 8, feat), F32), vm((doms, 8, feat), F32)]
        for _ in range(2):
            scratch += [dma((group,))] * 2 + [dma((doms,))] * 4 + [dma((group,))] * 2
        scratch += [dma((group,))] * 2 + [dma((doms,))] * 2
    in_vmem = pl.BlockSpec(memory_space=pltpu.VMEM)
    in_smem = pl.BlockSpec(memory_space=pltpu.SMEM)
    node_out, gsn, gb, gc = pl.pallas_call(
        functools.partial(kernel, cfg),
        out_shape=(
            jax.ShapeDtypeStruct((side, feat), BF16),
            jax.ShapeDtypeStruct((2 * feat, feat), F32),
            jax.ShapeDtypeStruct((8, feat), F32),
            jax.ShapeDtypeStruct((feat, cents), F32),
        ),
        in_specs=[in_vmem, in_vmem, in_vmem, in_smem, in_smem] + [in_vmem] * 4,
        out_specs=(in_vmem,) * 4,
        scratch_shapes=scratch,
        compiler_params=pltpu.CompilerParams(
            collective_id=0, has_side_effects=True, vmem_limit_bytes=50 * 1024 * 1024
        ),
    )(
        quantizer_codes.T,
        codebook.transpose(0, 2, 1).reshape(feat, cents),
        adj_tiles[0],
        tile_list[0],
        tile_count,
        w_self,
        w_neigh,
        out_bias.reshape(1, feat),
        cotangent,
    )
    grad_self, grad_neigh, grad_bias, grad_book = gsn[:feat], gsn[feat:], gb[0], gc
    if not reduce_here:
        grad_self, grad_neigh, grad_bias, grad_book = lax.psum(
            (grad_self, grad_neigh, jnp.sum(gb, axis=0), grad_book), ("dom", "tile", "rep")
        )
    return node_out, grad_self, grad_neigh, grad_bias, grad_book.reshape(subs, width, cents).transpose(0, 2, 1)


def solution(mesh):
    split = ("dom", "tile", "rep")
    in_specs = (P(split, None), P(), P(split, None, None, None), P(split, None, None), P(split), P(), P(), P(),
                P(split, None))
    out_specs = (P(split, None), P(), P(), P(), P())
    return jax.shard_map(body, mesh=mesh, in_specs=in_specs, out_specs=out_specs, check_vma=False)
```

time: 253 us -> 79.9 us (0.32)
  waiting for transfers between devices: 154 us -> 0 us
  Pallas kernels: 0 us -> 68.8 us
  blocking collectives: 53.8 us -> 0 us
  matrix products: 14.1 us -> 0 us
  between operations: 14.6 us -> 1.3 us
  starting transfers between devices: 3.89 us -> 0 us
    psum x1 -> x0, waiting for transfers between devices: 88.5 us -> none  [body(): lax.psum((grad_self, grad_neigh, grad_bias, grad_codebook), ('dom', 'tile...]
    pallas_call x0 -> x1, Pallas kernels: none -> 68.8 us  [body(): pl.pallas_call(functools.partial(kernel, cfg), out_shape=(jax.ShapeDtypeS...]
    psum x1 -> x0, blocking collectives: 37.7 us -> none  [body(): lax.psum((grad_self, grad_neigh, grad_bias, grad_codebook), ('dom', 'tile...]
    reduce_scatter x1 -> x0, waiting for transfers between devices: 26.1 us -> none  [body(): lax.psum_scatter(summed.reshape(lax.axis_size('dom') * tile_side, feat_wi...]
    all_gather x1 -> x0, waiting for transfers between devices: 25.7 us -> none  [body(): lax.all_gather(feats, ('tile', 'rep'), axis=0, tiled=True)]
    all_gather x1 -> x0, blocking collectives: 16 us -> none  [body(): lax.all_gather(dagg, 'dom', axis=0, tiled=True)]
    dot_general x12 -> x0, matrix products: 14.1 us -> none  [the longest x1 3.84 us: body(): jnp.einsum('nmk,nme->mke', own_onehot, input_gradient_total, precision=HI...]
    all_to_all x1 -> x0, waiting for transfers between devices: 13.5 us -> none  [body(): lax.all_to_all(column_low, ('tile', 'rep'), split_axis=0, concat_axis=0,...]
  transfers between devices with their start and end apart: 4 -> 0, of which waited for: 4 -> 0; matrix products, arithmetic and copies ran while one was open for 1% -> 0% of each run, Pallas kernels for 0% -> 0%
where the time goes in v1:
time: 79.9 us; the launch traced here: 79.6 us
  Pallas kernels  68.8 us (86%)
  local copies, waits for them, and re-layouts  9.51 us (12%)
  between operations  1.3 us (2%)
    pallas_call x1, Pallas kernels, body(): pl.pallas_call(functools.partial(kernel, cfg), out_shape=(jax.ShapeDtypeS...  68.8 us
    unnamed x18, local copies, waits for them, and re-layouts  8.03 us

profile of v1, /device:TPU:0, one launch (start us, length us, event | category | flops | bytes accessed | tf_op | source)
XLA Modules:
  0.0 79.6 jit_solution(18186119896483242665)
XLA Ops:
  1.3 0.0 copy-start.7
  1.3 0.7 copy-done.7
  2.0 0.0 copy-start.6
  2.0 0.1 copy.14.refs_3_
  2.1 0.6 copy-done.6
  2.6 0.0 copy-start
  2.6 1.0 %copy-done = bf16[1,4,256,256]{3,2,1,0:T(8,128)(2,1)S(1)} copy-done((bf16[1,4,256,256]{3,2,1,0:T(8,128)(2,1)S(1)}, bf16[1,4,256,256]{3,2,1,0:T(8,128)(2,1)}, u32[]{:S(2)}) %copy-start) | copy-done | bytes 524312
  3.7 0.0 copy-start.1
  3.7 0.9 %copy-done.1 = bf16[32,256,8]{1,2,0:T(8,128)(2,1)S(1)} copy-done((bf16[32,256,8]{1,2,0:T(8,128)(2,1)S(1)}, bf16[32,256,8]{1,2,0:T(8,128)(2,1)}, u32[]{:S(2)}) %copy-start.1) | copy-done | bytes 131096
  4.6 0.0 copy-start.2
  4.6 0.9 %copy-done.2 = bf16[256,256]{1,0:T(8,128)(2,1)S(1)} copy-done((bf16[256,256]{1,0:T(8,128)(2,1)S(1)}, bf16[256,256]{1,0:T(8,128)(2,1)}, u32[]{:S(2)}) %copy-start.2) | copy-done | bytes 131096
  5.5 0.0 copy-start.3
  5.5 0.9 %copy-done.3 = bf16[256,256]{1,0:T(8,128)(2,1)S(1)} copy-done((bf16[256,256]{1,0:T(8,128)(2,1)S(1)}, bf16[256,256]{1,0:T(8,128)(2,1)}, u32[]{:S(2)}) %copy-start.3) | copy-done | bytes 131096
  6.4 0.0 copy-start.4
  6.4 0.9 %copy-done.4 = bf16[256,256]{1,0:T(8,128)(2,1)S(1)} copy-done((bf16[256,256]{1,0:T(8,128)(2,1)S(1)}, bf16[256,256]{1,0:T(8,128)(2,1)}, u32[]{:S(2)}) %copy-start.4) | copy-done | bytes 131096
  7.3 0.0 copy-start.5
  7.3 0.8 copy-done.5
  8.1 68.8 %shard_map.128 = (bf16[256,256]{1,0:T(8,128)(2,1)S(1)}, f32[512,256]{1,0:T(8,128)S(1)}, f32[8,256]{1,0:T(8,128)S(1)}, f32[256,256]{1,0:T(8,128)S(1)}) custom-call(s32[32,256]{1,0:T(8,128)S(1)} %bitcast.14, bf16[256,256]{1,0:T(8,128)(2,1)S(1)} %bitcast.13, bf16[4,256,256]{2,1,0:T(8,128)(2,1)S(1)} %bitcast.11, s32[4,2]{1,0:T(4,128)S(1)} %copy.14.refs_3_, ...), custom_call_target="tpu_custom_call" | custom-call | tf_op jit(solution)/shard_map/pallas_call | solution.py:366
  76.8 0.6 slice.11
  77.4 0.8 %fusion = (f32[256,256]{1,0:T(8,128)}, f32[256,256]{1,0:T(8,128)}) fusion(f32[512,256]{1,0:T(8,128)S(1)} %get-tuple-element.10), kind=kLoop, calls=%fused_computation | loop fusion | bytes 1048576 | tf_op jit(solution)/shard_map/slice | solution.py:391
  78.2 0.7 copy.18
  78.9 0.7 copy.19
Async XLA Ops:
  1.3 0.7 copy-start.7
  2.0 0.7 copy-start.6
  2.6 1.0 %copy-start = (bf16[1,4,256,256]{3,2,1,0:T(8,128)(2,1)S(1)}, bf16[1,4,256,256]{3,2,1,0:T(8,128)(2,1)}, u32[]{:S(2)}) copy-start(bf16[1,4,256,256]{3,2,1,0:T(8,128)(2,1)} %param.11) | copy-start | bytes 1572868
  3.7 0.9 %copy-start.1 = (bf16[32,256,8]{1,2,0:T(8,128)(2,1)S(1)}, bf16[32,256,8]{1,2,0:T(8,128)(2,1)}, u32[]{:S(2)}) copy-start(bf16[32,256,8]{1,2,0:T(8,128)(2,1)} %param.10) | copy-start | bytes 393220
  4.6 0.9 %copy-start.2 = (bf16[256,256]{1,0:T(8,128)(2,1)S(1)}, bf16[256,256]{1,0:T(8,128)(2,1)}, u32[]{:S(2)}) copy-start(bf16[256,256]{1,0:T(8,128)(2,1)} %refs_5_.1) | copy-start | bytes 393220
  5.5 0.9 %copy-start.3 = (bf16[256,256]{1,0:T(8,128)(2,1)S(1)}, bf16[256,256]{1,0:T(8,128)(2,1)}, u32[]{:S(2)}) copy-start(bf16[256,256]{1,0:T(8,128)(2,1)} %refs_6_.1) | copy-start | bytes 393220
  6.4 0.9 %copy-start.4 = (bf16[256,256]{1,0:T(8,128)(2,1)S(1)}, bf16[256,256]{1,0:T(8,128)(2,1)}, u32[]{:S(2)}) copy-start(bf16[256,256]{1,0:T(8,128)(2,1)} %refs_8_.1) | copy-start | bytes 393220
  7.3 0.8 copy-start.5

commit v2 on v1

--- a/solution.py
+++ b/solution.py
@@ -12,6 +12,7 @@
 NN = (((1,), (0,)), ((), ()))
 NT = (((1,), (1,)), ((), ()))
 CHUNKS = 2
+LANES = 128
 ROWS16 = 16
 
 
@@ -32,12 +33,26 @@
     group = tiles * reps
     width = feat // subs
     part = side // CHUNKS
-    (codes_ref, book_ref, adj_ref, list_ref, count_ref, ws_ref, wn_ref, bias_ref, cot_ref) = refs[:9]
-    out_ref, gsn_ref, gb_ref, gc_ref = refs[9:13]
+    list_ref, count_ref = refs[:2]
+    sources = refs[2:9]
+    results = refs[9:13]
     (codes_all, codes_one, onehot, feats_t, slot_t, feats, self_act, part_own, part_send, part_recv,
      agg, dpre, dagg_0, dagg_1, back, dx, col_send, col_recv,
-     codes_s, codes_r, part_s, part_r, dagg_s, dagg_r, col_s, col_r) = refs[13:39]
-
+     codes_s, codes_r, part_s, part_r, dagg_s, dagg_r, col_s, col_r,
+     codes_ref, book_ref, adj_ref, ws_ref, wn_ref, bias_ref, cot_ref, in_sems, table,
+     out_ref, gsn_ref, gb_ref, gc_ref, out_sems) = refs[13:53]
+    loads = [
+        pltpu.make_async_copy(src, dst, in_sems.at[at])
+        for at, (src, dst) in enumerate(
+            zip(sources, (codes_ref, book_ref, adj_ref, ws_ref, wn_ref, bias_ref, cot_ref))
+        )
+    ]
+    for load in loads:
+        load.start()
+    stores = [
+        pltpu.make_async_copy(src, dst, out_sems.at[at])
+        for at, (src, dst) in enumerate(zip((out_ref, gsn_ref, gb_ref, gc_ref), results))
+    ]
     dagg_all = (dagg_0, dagg_1)
     d = lax.axis_index("dom")
     g = lax.axis_index("tile") * reps + lax.axis_index("rep")
@@ -64,8 +79,10 @@
     barrier = pltpu.get_barrier_semaphore()
     each(1, group, lambda k: pl.semaphore_signal(barrier, inc=1, device_id=group_peer(k)[1], device_id_type=MESH))
     each(1, doms, lambda k: pl.semaphore_signal(barrier, inc=1, device_id=dom_peer(k)[1], device_id_type=MESH))
+    loads[0].wait()
     codes_all[g] = codes_ref[...].astype(F32).astype(BF16)
-    codes_one[...] = codes_ref[...].astype(F32)
+    loads[1].wait()
+    table[...] = book_ref[...].astype(F32)
     pl.semaphore_wait(barrier, group + doms - 2)
 
     def codes_copy(k):
@@ -77,37 +94,43 @@
 
     each(1, group, lambda k: codes_copy(k).start())
 
-    cent_ids = lax.broadcasted_iota(jnp.int32, (cents, side), 0).astype(F32)
-
-    def decode(dst, keep):
+    def decode(codes, dst):
         def step(it, carry):
-            slab = codes_one[pl.ds(pl.multiple_of(it * 8, 8), 8), :]
-            for pair in range(4):
-                rows = pl.ds(pl.multiple_of(it * (8 * width) + pair * 2 * width, 16), 2 * width)
-                lhs = book_ref[rows, :]
-                halves = []
-                for odd in range(2):
-                    at = pair * 2 + odd
-                    hot = jnp.where(slab[at:at + 1, :] == cent_ids, 1.0, 0.0).astype(BF16)
-                    if keep:
-                        onehot[it * 8 + at] = hot
-                    halves.append(mm(lhs, hot)[odd * width:(odd + 1) * width, :])
-                dst[rows, :] = jnp.concatenate(halves, axis=0).astype(BF16)
+            slab = codes[pl.ds(pl.multiple_of(it * 8, 8), 8), :]
+            found = []
+            for at in range(8):
+                rows = pl.ds(pl.multiple_of(it * (8 * width) + at * width, 8), width)
+                ids = jnp.broadcast_to(slab[at:at + 1, :], (width, side))
+                across = []
+                for n in range(0, side, LANES):
+                    here = ids[:, n:n + LANES]
+                    low = here & (LANES - 1)
+                    value = jnp.take_along_axis(table[rows, 0:LANES], low, axis=1)
+                    for k in range(LANES, cents, LANES):
+                        other = jnp.take_along_axis(table[rows, k:k + LANES], low, axis=1)
+                        value = jnp.where(here >= k, other, value)
+                    across.append(value)
+                found.append(jnp.concatenate(across, axis=1))
+            dst[pl.ds(pl.multiple_of(it * (8 * width), 16), 8 * width), :] = (
+                jnp.concatenate(found, axis=0).astype(BF16)
+            )
             return carry
         lax.fori_loop(0, subs // 8, step, 0)
 
-    decode(feats_t, True)
+    decode(codes_ref, feats_t)
+    for load in loads[2:]:
+        load.wait()
     feats[...] = feats_t[...].astype(F32).T.astype(BF16)
     self_act[...] = mm(feats[...], ws_ref[...]) + bias_ref[...]
 
     live = [jnp.where(s < count_ref[0], 1.0, 0.0).astype(F32) for s in range(slots)]
-    row_dom = [lax.div(list_ref[s, 0], group) for s in range(slots)]
-    col_pos = [lax.rem(list_ref[s, 1], group) for s in range(slots)]
+    row_dom = [lax.div(list_ref[0, s], group) for s in range(slots)]
+    col_pos = [lax.rem(list_ref[1, s], group) for s in range(slots)]
 
     each(1, group, codes_wait)
     for s in range(slots):
-        codes_one[...] = codes_all[col_pos[s]].astype(F32)
-        decode(slot_t.at[s], False)
+        codes_one[...] = codes_all[col_pos[s]].astype(F32).astype(jnp.int32)
+        decode(codes_one, slot_t.at[s])
 
     def part_copy(c, k):
         return copy(part_send.at[c, k], part_recv.at[c, k], part_s.at[c, k], part_r.at[c, k], dom_peer(k)[1])
@@ -123,6 +146,16 @@
                 part_copy(c, k).start()
             else:
                 part_own[rows, :] = total
+
+    cent_ids = lax.broadcasted_iota(jnp.int32, (cents, side), 0)
+
+    def hot_step(it, carry):
+        slab = codes_ref[pl.ds(pl.multiple_of(it * 8, 8), 8), :]
+        for at in range(8):
+            onehot[it * 8 + at] = jnp.where(slab[at:at + 1, :] == cent_ids, 1.0, 0.0).astype(BF16)
+        return carry
+
+    lax.fori_loop(0, subs // 8, hot_step, 0)
 
     def dagg_copy(c, k):
         return copy(dagg_all[c].at[d], dagg_all[c].at[d], dagg_s.at[c, k], dagg_r.at[c, k], dom_peer(k)[1])
@@ -153,15 +186,17 @@
         for k in range(1, doms):
             dagg_copy(c, k).start()
 
+    stores[0].start()
+
     dpre_all = dpre[...]
     grad_self = mm(feats_t[...], dpre_all)
     grad_neigh = mm(agg[...].astype(F32).T.astype(BF16), dpre_all)
     grad_bias = jnp.sum(dpre_all.astype(F32).reshape(side // 8, 8, feat), axis=0)
 
     if reduce_here:
-        (gs, g_recv, g_mid, gz_recv, g_fin, cs, c_recv, c_mid, cz_recv, c_fin, b_grp, b_dom,
-         g1s, g1r, g2s, g2r, g3s, g3r, g4s, g4r, c1s, c1r, c2s, c2r, c3s, c3r, c4s, c4r,
-         b1s, b1r, b2s, b2r) = refs[39:]
+        (gs, g_recv, g_mid, g_fin, cs, c_recv, c_mid, c_fin, b_grp, b_dom,
+         g1s, g1r, g2s, g2r, g4s, g4r, c1s, c1r, c2s, c2r, c4s, c4r,
+         b1s, b1r, b2s, b2r) = refs[53:]
 
         def rs_group(src, dst, ss, rr):
             def go(k):
@@ -169,12 +204,6 @@
                 return copy(src.at[p], dst.at[k], ss.at[k], rr.at[k], device)
             return go
 
-        def rs_dom(src, dst, ss, rr):
-            def go(k):
-                p, device = dom_peer(k)
-                return copy(src.at[p], dst.at[k], ss.at[k], rr.at[k], device)
-            return go
-
         def ag_dom(own, slot, ss, rr):
             def go(k):
                 return copy(own, own, ss.at[k], rr.at[k], dom_peer(k)[1])
@@ -201,26 +230,26 @@
             sends.append((go, n))
 
         g1 = rs_group(gs, g_recv, g1s, g1r)
-        g2 = rs_dom(g_mid, gz_recv, g2s, g2r)
-        g3 = ag_dom(g_fin.at[g, d], lambda at: g_fin.at[g, at], g3s, g3r)
+        g2 = ag_dom(g_mid.at[d], lambda at: g_mid.at[at], g2s, g2r)
         g4 = ag_group(g_fin, g4s, g4r)
         c1 = rs_group(cs, c_recv, c1s, c1r)
-        c2 = rs_dom(c_mid, cz_recv, c2s, c2r)
-        c3 = ag_dom(c_fin.at[g, d], lambda at: c_fin.at[g, at], c3s, c3r)
+        c2 = ag_dom(c_mid.at[d], lambda at: c_mid.at[at], c2s, c2r)
         c4 = ag_group(c_fin, c4s, c4r)
         b1 = ag_group(b_grp, b1s, b1r)
         b2 = ag_dom(b_dom.at[d], lambda at: b_dom.at[at], b2s, b2r)
 
         half = group // 2
-        gs[0:half] = grad_self.astype(BF16).reshape(half, doms, ROWS16, feat)
-        gs[half:group] = grad_neigh.astype(BF16).reshape(half, doms, ROWS16, feat)
+        gs[0:half] = grad_self.astype(BF16).reshape(half, 2 * feat // group, feat)
+        gs[half:group] = grad_neigh.astype(BF16).reshape(half, 2 * feat // group, feat)
         b_grp[g] = grad_bias
         start(g1, group)
         start(b1[0], group)
     else:
         gsn_ref[0:feat, :] = grad_self
         gsn_ref[feat:2 * feat, :] = grad_neigh
-        gb_ref[...] = grad_bias
+        gb_ref[...] = jnp.broadcast_to(jnp.sum(grad_bias, axis=0, keepdims=True), (8, feat))
+        stores[1].start()
+        stores[2].start()
 
     dx[...] = mm(ws_ref[...], dpre_all, NT)
 
@@ -250,20 +279,15 @@
         for k in range(1, group):
             g1(k).wait_recv()
             mid = mid + g_recv[k].astype(F32)
-        g_mid[...] = mid.astype(BF16)
-        start(g2, doms)
+        g_mid[d] = mid.astype(BF16)
+        start(g2[0], doms)
         for k in range(1, group):
             b1[1](k)
         b_dom[d] = jnp.sum(b_grp[...], axis=0)
         start(b2[0], doms)
-        fin = g_mid[d].astype(F32)
-        for k in range(1, doms):
-            g2(k).wait_recv()
-            fin = fin + gz_recv[k].astype(F32)
-        g_fin[g, d] = fin.astype(BF16)
-        start(g3[0], doms)
-        for k in range(1, doms):
-            g3[1](k)
+        for k in range(1, doms):
+            g2[1](k)
+        g_fin[g] = jnp.sum(g_mid[...].astype(F32), axis=0).astype(BF16)
         start(g4[0], group)
 
     def add_column(k):
@@ -288,7 +312,7 @@
         lanes = cents // 2
         for h in range(2):
             cs[h * half:(h + 1) * half] = (
-                gc_ref[:, h * lanes:(h + 1) * lanes].astype(BF16).reshape(half, doms, ROWS16, lanes)
+                gc_ref[:, h * lanes:(h + 1) * lanes].astype(BF16).reshape(half, 2 * feat // group, lanes)
             )
         start(c1, group)
         for k in range(1, group):
@@ -297,20 +321,17 @@
         for k in range(1, doms):
             b2[1](k)
         gb_ref[...] = jnp.broadcast_to(jnp.sum(jnp.sum(b_dom[...], axis=0), axis=0, keepdims=True), (8, feat))
+        stores[1].start()
+        stores[2].start()
         mid = cs[g].astype(F32)
         for k in range(1, group):
             c1(k).wait_recv()
             mid = mid + c_recv[k].astype(F32)
-        c_mid[...] = mid.astype(BF16)
-        start(c2, doms)
-        fin = c_mid[d].astype(F32)
-        for k in range(1, doms):
-            c2(k).wait_recv()
-            fin = fin + cz_recv[k].astype(F32)
-        c_fin[g, d] = fin.astype(BF16)
-        start(c3[0], doms)
-        for k in range(1, doms):
-            c3[1](k)
+        c_mid[d] = mid.astype(BF16)
+        start(c2[0], doms)
+        for k in range(1, doms):
+            c2[1](k)
+        c_fin[g] = jnp.sum(c_mid[...].astype(F32), axis=0).astype(BF16)
         start(c4[0], group)
         for k in range(1, group):
             c4[1](k)
@@ -318,6 +339,8 @@
             gc_ref[:, h * lanes:(h + 1) * lanes] = (
                 c_fin[h * half:(h + 1) * half].astype(F32).reshape(feat, lanes)
             )
+    stores[3].start()
+    if reduce_here:
         for go, n in sends:
             for k in range(1, n):
                 go(k).wait_send()
@@ -328,6 +351,24 @@
         for k in range(1, doms):
             part_copy(c, k).wait_send()
             dagg_copy(c, k).wait_send()
+    for store in stores:
+        store.wait()
+
+
+def write_out(node_ref, gsn_ref, gb_ref, gc_ref, node_hbm, self_hbm, neigh_hbm, bias_hbm, book_hbm, sems):
+    feat = self_hbm.shape[0]
+    pairs = (
+        (gsn_ref.at[pl.ds(0, feat)], self_hbm),
+        (gsn_ref.at[pl.ds(feat, feat)], neigh_hbm),
+        (gc_ref, book_hbm),
+        (node_ref, node_hbm),
+        (gb_ref.at[pl.ds(0, 1)], bias_hbm),
+    )
+    copies = [pltpu.make_async_copy(src, dst, sems.at[at]) for at, (src, dst) in enumerate(pairs)]
+    for copy in copies:
+        copy.start()
+    for copy in copies:
+        copy.wait()
 
 
 def body(quantizer_codes, codebook, adj_tiles, tile_list, tile_count, w_self, w_neigh, out_bias, cotangent):
@@ -337,11 +378,11 @@
     feat = subs * width
     slots, side = adj_tiles.shape[1], adj_tiles.shape[2]
     part = side // CHUNKS
-    reduce_here = group % 2 == 0 and group * doms * ROWS16 == 2 * feat and feat == cents
+    reduce_here = group % 2 == 0 and 2 * feat % (group * ROWS16) == 0 and feat == cents and group <= 8
     cfg = (doms, tiles, reps, slots, side, feat, subs, cents, reduce_here)
     vm, dma = pltpu.VMEM, pltpu.SemaphoreType.DMA
     scratch = [
-        vm((group, subs, side), BF16), vm((subs, side), F32), vm((subs, cents, side), BF16),
+        vm((group, subs, side), BF16), vm((subs, side), jnp.int32), vm((subs, cents, side), BF16),
         vm((feat, side), BF16), vm((slots, feat, side), BF16), vm((side, feat), BF16), vm((side, feat), F32),
         vm((side, feat), F32), vm((CHUNKS, doms, part, feat), BF16), vm((CHUNKS, doms, part, feat), BF16),
         vm((side, feat), BF16), vm((side, feat), BF16), vm((doms, feat, part), BF16), vm((doms, feat, part), BF16),
@@ -349,20 +390,23 @@
         vm((group, feat, side), BF16), vm((group, feat, side), BF16),
         dma((group,)), dma((group,)), dma((CHUNKS, doms)), dma((CHUNKS, doms)),
         dma((CHUNKS, doms)), dma((CHUNKS, doms)), dma((group,)), dma((group,)),
+        vm((subs, side), jnp.int32), vm((feat, cents), BF16), vm((slots, side, side), BF16), vm((feat, feat), BF16),
+        vm((feat, feat), BF16), vm((1, feat), F32), vm((side, feat), BF16), dma((7,)), vm((feat, cents), F32),
+        vm((side, feat), BF16), vm((2 * feat, feat), F32), vm((8, feat), F32), vm((feat, cents), F32), dma((4,)),
     ]
     if reduce_here:
         for lanes in (feat, cents // 2):
+            piece = 2 * feat // group
             scratch += [
-                vm((group, doms, ROWS16, lanes), BF16), vm((group, doms, ROWS16, lanes), BF16),
-                vm((doms, ROWS16, lanes), BF16), vm((doms, ROWS16, lanes), BF16),
-                vm((group, doms, ROWS16, lanes), BF16),
+                vm((group, piece, lanes), BF16), vm((group, piece, lanes), BF16),
+                vm((doms, piece, lanes), BF16), vm((group, piece, lanes), BF16),
             ]
         scratch += [vm((group, 8, feat), F32), vm((doms, 8, feat), F32)]
         for _ in range(2):
-            scratch += [dma((group,))] * 2 + [dma((doms,))] * 4 + [dma((group,))] * 2
+            scratch += [dma((group,))] * 2 + [dma((doms,))] * 2 + [dma((group,))] * 2
         scratch += [dma((group,))] * 2 + [dma((doms,))] * 2
-    in_vmem = pl.BlockSpec(memory_space=pltpu.VMEM)
     in_smem = pl.BlockSpec(memory_space=pltpu.SMEM)
+    in_hbm = pl.BlockSpec(memory_space=pltpu.HBM)
     node_out, gsn, gb, gc = pl.pallas_call(
         functools.partial(kernel, cfg),
         out_shape=(
@@ -371,27 +415,41 @@
             jax.ShapeDtypeStruct((8, feat), F32),
             jax.ShapeDtypeStruct((feat, cents), F32),
         ),
-        in_specs=[in_vmem, in_vmem, in_vmem, in_smem, in_smem] + [in_vmem] * 4,
-        out_specs=(in_vmem,) * 4,
+        in_specs=[in_smem] * 2 + [in_hbm] * 7,
+        out_specs=(in_hbm,) * 4,
         scratch_shapes=scratch,
         compiler_params=pltpu.CompilerParams(
-            collective_id=0, has_side_effects=True, vmem_limit_bytes=50 * 1024 * 1024
+            collective_id=0, has_side_effects=True, vmem_limit_bytes=58 * 1024 * 1024
         ),
     )(
+        tile_list[0].T,
+        tile_count,
         quantizer_codes.T,
         codebook.transpose(0, 2, 1).reshape(feat, cents),
         adj_tiles[0],
-        tile_list[0],
-        tile_count,
         w_self,
         w_neigh,
         out_bias.reshape(1, feat),
         cotangent,
     )
-    grad_self, grad_neigh, grad_bias, grad_book = gsn[:feat], gsn[feat:], gb[0], gc
+    node_out, grad_self, grad_neigh, grad_bias, grad_book = pl.pallas_call(
+        write_out,
+        out_shape=(
+            jax.ShapeDtypeStruct((side, feat), BF16),
+            jax.ShapeDtypeStruct((feat, feat), F32),
+            jax.ShapeDtypeStruct((feat, feat), F32),
+            jax.ShapeDtypeStruct((1, feat), F32),
+            jax.ShapeDtypeStruct((feat, cents), F32),
+        ),
+        in_specs=[in_hbm] * 4,
+        out_specs=(in_hbm,) * 5,
+        scratch_shapes=[dma((5,))],
+        compiler_params=pltpu.CompilerParams(vmem_limit_bytes=58 * 1024 * 1024),
+    )(node_out, gsn, gb, gc)
+    grad_bias = grad_bias[0]
     if not reduce_here:
         grad_self, grad_neigh, grad_bias, grad_book = lax.psum(
-            (grad_self, grad_neigh, jnp.sum(gb, axis=0), grad_book), ("dom", "tile", "rep")
+            (grad_self, grad_neigh, grad_bias, grad_book), ("dom", "tile", "rep")
         )
     return node_out, grad_self, grad_neigh, grad_bias, grad_book.reshape(subs, width, cents).transpose(0, 2, 1)
 

time: 79.9 us -> 95.2 us (1.19)
  Pallas kernels: 68.8 us -> 93.8 us
  local copies, waits for them, and re-layouts: 9.51 us -> 0 us
    pallas_call x0 -> x1, Pallas kernels: none -> 29 us  [body(): pl.pallas_call(write_out, out_shape=(jax.ShapeDtypeStruct((side, feat), B...]
    unnamed x18 -> x0, local copies, waits for them, and re-layouts: 8.03 us -> none
    pallas_call x1, Pallas kernels: 68.8 us -> 64.8 us  [body(): pl.pallas_call(functools.partial(kernel, cfg), out_shape=(jax.ShapeDtypeS...]
    slice x2 -> x0, local copies, waits for them, and re-layouts: 1.39 us -> none  [the longest x1 0.82 us: body(): gsn[feat:]]
where the time goes in v2:
time: 95.2 us; the launch traced here: 95 us
  Pallas kernels  93.8 us (99%)
  between operations  1.29 us (1%)
    pallas_call x1, Pallas kernels, body(): pl.pallas_call(functools.partial(kernel, cfg), out_shape=(jax.ShapeDtypeS...  64.8 us
    pallas_call x1, Pallas kernels, body(): pl.pallas_call(write_out, out_shape=(jax.ShapeDtypeStruct((side, feat), B...  29 us

profile of v2, /device:TPU:0, one launch (start us, length us, event | category | flops | bytes accessed | tf_op | source)
XLA Modules:
  0.0 95.0 jit_solution(2932155631364160841)
XLA Ops:
  1.3 64.8 %shard_map.128 = (bf16[256,256]{1,0:T(8,128)(2,1)}, f32[512,256]{1,0:T(8,128)}, f32[8,256]{1,0:T(8,128)}, f32[256,256]{1,0:T(8,128)}) custom-call(s32[2,4]{1,0:T(2,128)} %bitcast.16, s32[1]{0:T(128)S(6)} %copy.14.refs_1_, s32[32,256]{1,0:T(8,128)} %bitcast.15, bf16[256,256]{1,0:T(8,128)(2,1)} %bitcast.14, bf16[4,256,256]{2,1,0:T(8,128)(2,1)} %bitcast.13, ...), custom_call_target="tpu_custom_call" | custom-call | tf_op jit(solution)/shard_map/pallas_call | solution.py:410
  66.1 29.0 %shard_map.129 = (bf16[256,256]{1,0:T(8,128)(2,1)}, f32[256,256]{1,0:T(8,128)}, f32[256,256]{1,0:T(8,128)}, f32[1,256]{1,0:T(1,128)}, f32[256,256]{1,0:T(8,128)}) custom-call(bf16[256,256]{1,0:T(8,128)(2,1)} %get-tuple-element.14.node_ref, f32[512,256]{1,0:T(8,128)} %get-tuple-element.15.gsn_ref, f32[8,256]{1,0:T(8,128)} %get-tuple-element.16.gb_ref, ...), custom_call_target="tpu_custom_call" | custom-call | tf_op jit(solution)/shard_map/pallas_call | solution.py:435

commit v3 on v2

--- a/solution.py
+++ b/solution.py
@@ -12,6 +12,7 @@
 NN = (((1,), (0,)), ((), ()))
 NT = (((1,), (1,)), ((), ()))
 CHUNKS = 2
+PARTS = 4
 LANES = 128
 ROWS16 = 16
 
@@ -37,10 +38,10 @@
     sources = refs[2:9]
     results = refs[9:13]
     (codes_all, codes_one, onehot, feats_t, slot_t, feats, self_act, part_own, part_send, part_recv,
-     agg, dpre, dagg_0, dagg_1, back, dx, col_send, col_recv,
+     agg, dpre, dagg_0, dagg_1, dagg_2, dagg_3, dx, col_send, col_recv,
      codes_s, codes_r, part_s, part_r, dagg_s, dagg_r, col_s, col_r,
      codes_ref, book_ref, adj_ref, ws_ref, wn_ref, bias_ref, cot_ref, in_sems, table,
-     out_ref, gsn_ref, gb_ref, gc_ref, out_sems) = refs[13:53]
+     out_ref, gsn_ref, gb_ref, gc_ref, out_sems) = refs[13:54]
     loads = [
         pltpu.make_async_copy(src, dst, in_sems.at[at])
         for at, (src, dst) in enumerate(
@@ -53,7 +54,7 @@
         pltpu.make_async_copy(src, dst, out_sems.at[at])
         for at, (src, dst) in enumerate(zip((out_ref, gsn_ref, gb_ref, gc_ref), results))
     ]
-    dagg_all = (dagg_0, dagg_1)
+    dagg_all = (dagg_0, dagg_1, dagg_2, dagg_3)
     d = lax.axis_index("dom")
     g = lax.axis_index("tile") * reps + lax.axis_index("rep")
 
@@ -182,13 +183,15 @@
         dhid = scale * cot - hidden * (scale * scale * scale * along)
         grad = (dhid * (sig * (1.0 + pre * (1.0 - sig)))).astype(BF16)
         dpre[rows, :] = grad
-        dagg_all[c][d] = mm(wn_ref[...], grad, NT).astype(BF16)
+
+    dpre_all = dpre[...]
+    fpart = feat // PARTS
+    for c in range(PARTS):
+        dagg_all[c][d] = mm(wn_ref[c * fpart:(c + 1) * fpart, :], dpre_all, NT).astype(BF16)
         for k in range(1, doms):
             dagg_copy(c, k).start()
-
     stores[0].start()
 
-    dpre_all = dpre[...]
     grad_self = mm(feats_t[...], dpre_all)
     grad_neigh = mm(agg[...].astype(F32).T.astype(BF16), dpre_all)
     grad_bias = jnp.sum(dpre_all.astype(F32).reshape(side // 8, 8, feat), axis=0)
@@ -196,7 +199,7 @@
     if reduce_here:
         (gs, g_recv, g_mid, g_fin, cs, c_recv, c_mid, c_fin, b_grp, b_dom,
          g1s, g1r, g2s, g2r, g4s, g4r, c1s, c1r, c2s, c2r, c4s, c4r,
-         b1s, b1r, b2s, b2r) = refs[53:]
+         b1s, b1r, b2s, b2r) = refs[54:]
 
         def rs_group(src, dst, ss, rr):
             def go(k):
@@ -232,7 +235,11 @@
         g1 = rs_group(gs, g_recv, g1s, g1r)
         g2 = ag_dom(g_mid.at[d], lambda at: g_mid.at[at], g2s, g2r)
         g4 = ag_group(g_fin, g4s, g4r)
-        c1 = rs_group(cs, c_recv, c1s, c1r)
+
+        def code_copy(c, k):
+            p, device = group_peer(k)
+            return copy(cs.at[c, p], c_recv.at[c, k], c1s.at[c, k], c1r.at[c, k], device)
+
         c2 = ag_dom(c_mid.at[d], lambda at: c_mid.at[at], c2s, c2r)
         c4 = ag_group(c_fin, c4s, c4r)
         b1 = ag_group(b_grp, b1s, b1r)
@@ -253,26 +260,25 @@
 
     dx[...] = mm(ws_ref[...], dpre_all, NT)
 
-    for c in range(CHUNKS):
+    def col_copy(c, k):
+        return copy(col_send.at[k, c], col_recv.at[k, c], col_s.at[c, k], col_r.at[c, k], group_peer(k)[1])
+
+    for c in range(PARTS):
+        rows = slice(c * fpart, (c + 1) * fpart)
         for k in range(1, doms):
             dagg_wait(c, k)
-        for s in range(slots):
-            prod = mm(dagg_all[c][row_dom[s]], adj_ref[s, c * part:(c + 1) * part, :]) * live[s]
-            back[s] = prod if c == 0 else back[s] + prod
-
-    def col_copy(k):
-        return copy(col_send.at[k], col_recv.at[k], col_s.at[k], col_r.at[k], group_peer(k)[1])
-
-    def column(k):
-        to = group_peer(k)[0]
-        return sum(back[s] * jnp.where(col_pos[s] == to, 1.0, 0.0).astype(F32) for s in range(slots))
-
-    def send_column(k):
-        col_send[k] = column(k).astype(BF16)
-        col_copy(k).start()
-
-    each(1, group, send_column)
-    dx[...] = dx[...] + column(0)
+        prods = [mm(dagg_all[c][row_dom[s]], adj_ref[s]) * live[s] for s in range(slots)]
+
+        def column(k):
+            to = group_peer(k)[0]
+            return sum(prods[s] * jnp.where(col_pos[s] == to, 1.0, 0.0).astype(F32) for s in range(slots))
+
+        def send_column(k):
+            col_send[k, c] = column(k).astype(BF16)
+            col_copy(c, k).start()
+
+        each(1, group, send_column)
+        dx[rows, :] = dx[rows, :] + column(0)
 
     if reduce_here:
         mid = gs[g].astype(F32)
@@ -285,36 +291,44 @@
             b1[1](k)
         b_dom[d] = jnp.sum(b_grp[...], axis=0)
         start(b2[0], doms)
-        for k in range(1, doms):
-            g2[1](k)
-        g_fin[g] = jnp.sum(g_mid[...].astype(F32), axis=0).astype(BF16)
-        start(g4[0], group)
-
-    def add_column(k):
-        col_copy(k).wait_recv()
-        dx[...] = dx[...] + col_recv[k].astype(F32)
-
-    each(1, group, add_column)
-
-    def code_step(it, carry):
-        for at in range(8):
-            rows = pl.ds(pl.multiple_of(it * (8 * width) + at * width, 8), width)
+
+    lanes = cents // 2
+    for c in range(PARTS):
+        base = c * fpart
+
+        def add_column(k):
+            col_copy(c, k).wait_recv()
+            dx[base:base + fpart, :] = dx[base:base + fpart, :] + col_recv[k, c].astype(F32)
+
+        each(1, group, add_column)
+        for at in range(fpart // width):
+            rows = slice(base + at * width, base + (at + 1) * width)
             full = dx[rows, :]
             high = full.astype(BF16).astype(F32)
             both = jnp.concatenate([high, full - high], axis=0).astype(BF16)
-            two = mm(both, onehot[it * 8 + at], NT)
+            two = mm(both, onehot[c * (fpart // width) + at], NT)
             gc_ref[rows, :] = two[0:width, :] + two[width:2 * width, :]
-        return carry
-
-    lax.fori_loop(0, subs // 8, code_step, 0)
+        if reduce_here:
+            for h in range(2):
+                cs[c, h * half:(h + 1) * half] = (
+                    gc_ref[base:base + fpart, h * lanes:(h + 1) * lanes].astype(BF16).reshape(half, fpart // half, lanes)
+                )
+            for k in range(1, group):
+                code_copy(c, k).start()
+            if c == 1:
+                for k in range(1, doms):
+                    g2[1](k)
+                g_fin[g] = jnp.sum(g_mid[...].astype(F32), axis=0).astype(BF16)
+                start(g4[0], group)
 
     if reduce_here:
-        lanes = cents // 2
-        for h in range(2):
-            cs[h * half:(h + 1) * half] = (
-                gc_ref[:, h * lanes:(h + 1) * lanes].astype(BF16).reshape(half, 2 * feat // group, lanes)
-            )
-        start(c1, group)
+        for c in range(PARTS):
+            mid = cs[c, g].astype(F32)
+            for k in range(1, group):
+                code_copy(c, k).wait_recv()
+                mid = mid + c_recv[c, k].astype(F32)
+            c_mid[d, c] = mid.astype(BF16)
+        start(c2[0], doms)
         for k in range(1, group):
             g4[1](k)
         gsn_ref[...] = g_fin[...].astype(F32).reshape(2 * feat, feat)
@@ -323,12 +337,6 @@
         gb_ref[...] = jnp.broadcast_to(jnp.sum(jnp.sum(b_dom[...], axis=0), axis=0, keepdims=True), (8, feat))
         stores[1].start()
         stores[2].start()
-        mid = cs[g].astype(F32)
-        for k in range(1, group):
-            c1(k).wait_recv()
-            mid = mid + c_recv[k].astype(F32)
-        c_mid[d] = mid.astype(BF16)
-        start(c2[0], doms)
         for k in range(1, doms):
             c2[1](k)
         c_fin[g] = jnp.sum(c_mid[...].astype(F32), axis=0).astype(BF16)
@@ -336,39 +344,45 @@
         for k in range(1, group):
             c4[1](k)
         for h in range(2):
-            gc_ref[:, h * lanes:(h + 1) * lanes] = (
-                c_fin[h * half:(h + 1) * half].astype(F32).reshape(feat, lanes)
-            )
+            for c in range(PARTS):
+                gc_ref[c * fpart:(c + 1) * fpart, h * lanes:(h + 1) * lanes] = (
+                    c_fin[h * half:(h + 1) * half, c].astype(F32).reshape(fpart, lanes)
+                )
     stores[3].start()
     if reduce_here:
         for go, n in sends:
             for k in range(1, n):
                 go(k).wait_send()
+        for c in range(PARTS):
+            for k in range(1, group):
+                code_copy(c, k).wait_send()
 
     each(1, group, lambda k: codes_copy(k).wait_send())
-    each(1, group, lambda k: col_copy(k).wait_send())
+    for c in range(PARTS):
+        each(1, group, functools.partial(lambda c, k: col_copy(c, k).wait_send(), c))
+        for k in range(1, doms):
+            dagg_copy(c, k).wait_send()
     for c in range(CHUNKS):
         for k in range(1, doms):
             part_copy(c, k).wait_send()
-            dagg_copy(c, k).wait_send()
     for store in stores:
         store.wait()
 
 
-def write_out(node_ref, gsn_ref, gb_ref, gc_ref, node_hbm, self_hbm, neigh_hbm, bias_hbm, book_hbm, sems):
+def write_out(node_in, gsn_in, gb_in, gc_in, node_hbm, self_hbm, neigh_hbm, bias_hbm, book_hbm, *scratch):
     feat = self_hbm.shape[0]
-    pairs = (
-        (gsn_ref.at[pl.ds(0, feat)], self_hbm),
-        (gsn_ref.at[pl.ds(feat, feat)], neigh_hbm),
-        (gc_ref, book_hbm),
-        (node_ref, node_hbm),
-        (gb_ref.at[pl.ds(0, 1)], bias_hbm),
-    )
-    copies = [pltpu.make_async_copy(src, dst, sems.at[at]) for at, (src, dst) in enumerate(pairs)]
-    for copy in copies:
-        copy.start()
-    for copy in copies:
-        copy.wait()
+    here, in_sems, out_sems = scratch[:5], scratch[5], scratch[6]
+    sources = (gsn_in.at[pl.ds(0, feat)], gsn_in.at[pl.ds(feat, feat)], gc_in, node_in, gb_in.at[pl.ds(0, 1)])
+    targets = (self_hbm, neigh_hbm, book_hbm, node_hbm, bias_hbm)
+    loads = [pltpu.make_async_copy(src, mid, in_sems.at[at]) for at, (src, mid) in enumerate(zip(sources, here))]
+    stores = [pltpu.make_async_copy(mid, dst, out_sems.at[at]) for at, (mid, dst) in enumerate(zip(here, targets))]
+    for load in loads:
+        load.start()
+    for load, store in zip(loads, stores):
+        load.wait()
+        store.start()
+    for store in stores:
+        store.wait()
 
 
 def body(quantizer_codes, codebook, adj_tiles, tile_list, tile_count, w_self, w_neigh, out_bias, cotangent):
@@ -378,32 +392,33 @@
     feat = subs * width
     slots, side = adj_tiles.shape[1], adj_tiles.shape[2]
     part = side // CHUNKS
-    reduce_here = group % 2 == 0 and 2 * feat % (group * ROWS16) == 0 and feat == cents and group <= 8
+    reduce_here = group % 2 == 0 and 2 * feat % (group * PARTS * ROWS16) == 0 and feat == cents and group <= 8
     cfg = (doms, tiles, reps, slots, side, feat, subs, cents, reduce_here)
     vm, dma = pltpu.VMEM, pltpu.SemaphoreType.DMA
     scratch = [
         vm((group, subs, side), BF16), vm((subs, side), jnp.int32), vm((subs, cents, side), BF16),
         vm((feat, side), BF16), vm((slots, feat, side), BF16), vm((side, feat), BF16), vm((side, feat), F32),
         vm((side, feat), F32), vm((CHUNKS, doms, part, feat), BF16), vm((CHUNKS, doms, part, feat), BF16),
-        vm((side, feat), BF16), vm((side, feat), BF16), vm((doms, feat, part), BF16), vm((doms, feat, part), BF16),
-        vm((slots, feat, side), F32), vm((feat, side), F32),
-        vm((group, feat, side), BF16), vm((group, feat, side), BF16),
+        vm((side, feat), BF16), vm((side, feat), BF16), *[vm((doms, feat // PARTS, side), BF16)] * PARTS, vm((feat, side), F32),
+        vm((group, PARTS, feat // PARTS, side), BF16), vm((group, PARTS, feat // PARTS, side), BF16),
         dma((group,)), dma((group,)), dma((CHUNKS, doms)), dma((CHUNKS, doms)),
-        dma((CHUNKS, doms)), dma((CHUNKS, doms)), dma((group,)), dma((group,)),
+        dma((PARTS, doms)), dma((PARTS, doms)), dma((PARTS, group)), dma((PARTS, group)),
         vm((subs, side), jnp.int32), vm((feat, cents), BF16), vm((slots, side, side), BF16), vm((feat, feat), BF16),
         vm((feat, feat), BF16), vm((1, feat), F32), vm((side, feat), BF16), dma((7,)), vm((feat, cents), F32),
         vm((side, feat), BF16), vm((2 * feat, feat), F32), vm((8, feat), F32), vm((feat, cents), F32), dma((4,)),
     ]
     if reduce_here:
-        for lanes in (feat, cents // 2):
-            piece = 2 * feat // group
-            scratch += [
-                vm((group, piece, lanes), BF16), vm((group, piece, lanes), BF16),
-                vm((doms, piece, lanes), BF16), vm((group, piece, lanes), BF16),
-            ]
+        piece, lanes = 2 * feat // group, cents // 2
+        some = 2 * feat // PARTS // group
+        scratch += [
+            vm((group, piece, feat), BF16), vm((group, piece, feat), BF16),
+            vm((doms, piece, feat), BF16), vm((group, piece, feat), BF16),
+            vm((PARTS, group, some, lanes), BF16), vm((PARTS, group, some, lanes), BF16),
+            vm((doms, PARTS, some, lanes), BF16), vm((group, PARTS, some, lanes), BF16),
+        ]
         scratch += [vm((group, 8, feat), F32), vm((doms, 8, feat), F32)]
-        for _ in range(2):
-            scratch += [dma((group,))] * 2 + [dma((doms,))] * 2 + [dma((group,))] * 2
+        for first in ((group,), (PARTS, group)):
+            scratch += [dma(first)] * 2 + [dma((doms,))] * 2 + [dma((group,))] * 2
         scratch += [dma((group,))] * 2 + [dma((doms,))] * 2
     in_smem = pl.BlockSpec(memory_space=pltpu.SMEM)
     in_hbm = pl.BlockSpec(memory_space=pltpu.HBM)
@@ -443,7 +458,10 @@
         ),
         in_specs=[in_hbm] * 4,
         out_specs=(in_hbm,) * 5,
-        scratch_shapes=[dma((5,))],
+        scratch_shapes=[
+            vm((feat, feat), F32), vm((feat, feat), F32), vm((feat, cents), F32), vm((side, feat), BF16),
+            vm((1, feat), F32), dma((5,)), dma((5,)),
+        ],
         compiler_params=pltpu.CompilerParams(vmem_limit_bytes=58 * 1024 * 1024),
     )(node_out, gsn, gb, gc)
     grad_bias = grad_bias[0]

time: 95.2 us -> 63.7 us (0.67)
  Pallas kernels: 93.8 us -> 62.2 us
    pallas_call x1, Pallas kernels: 29 us -> 1.95 us  [body(): pl.pallas_call(write_out, out_shape=(jax.ShapeDtypeStruct((side, feat), B...]
    pallas_call x1, Pallas kernels: 64.8 us -> 60.3 us  [body(): pl.pallas_call(functools.partial(kernel, cfg), out_shape=(jax.ShapeDtypeS...]
where the time goes in v3:
time: 63.7 us; the launch traced here: 63.5 us
  Pallas kernels  62.2 us (98%)
  between operations  1.29 us (2%)
    pallas_call x1, Pallas kernels, body(): pl.pallas_call(functools.partial(kernel, cfg), out_shape=(jax.ShapeDtypeS...  60.3 us
    pallas_call x1, Pallas kernels, body(): pl.pallas_call(write_out, out_shape=(jax.ShapeDtypeStruct((side, feat), B...  1.95 us

profile of v3, /device:TPU:0, one launch (start us, length us, event | category | flops | bytes accessed | tf_op | source)
XLA Modules:
  0.0 63.5 jit_solution(8375906125493587083)
XLA Ops:
  1.3 60.3 %shard_map.128 = (bf16[256,256]{1,0:T(8,128)(2,1)}, f32[512,256]{1,0:T(8,128)}, f32[8,256]{1,0:T(8,128)}, f32[256,256]{1,0:T(8,128)}) custom-call(s32[2,4]{1,0:T(2,128)} %bitcast.16, s32[1]{0:T(128)S(6)} %copy.14.refs_1_, s32[32,256]{1,0:T(8,128)} %bitcast.15, bf16[256,256]{1,0:T(8,128)(2,1)} %bitcast.14, bf16[4,256,256]{2,1,0:T(8,128)(2,1)} %bitcast.13, ...), custom_call_target="tpu_custom_call" | custom-call | tf_op jit(solution)/shard_map/pallas_call | solution.py:425
  61.6 2.0 %shard_map.129 = (bf16[256,256]{1,0:T(8,128)(2,1)}, f32[256,256]{1,0:T(8,128)}, f32[256,256]{1,0:T(8,128)}, f32[1,256]{1,0:T(1,128)}, f32[256,256]{1,0:T(8,128)}) custom-call(bf16[256,256]{1,0:T(8,128)(2,1)} %get-tuple-element.14.node_in, f32[512,256]{1,0:T(8,128)} %get-tuple-element.15.gsn_in, f32[8,256]{1,0:T(8,128)} %get-tuple-element.16.gb_in, ...), custom_call_target="tpu_custom_call" | custom-call | tf_op jit(solution)/shard_map/pallas_call | solution.py:450

commit v4 on v3

--- a/solution.py
+++ b/solution.py
@@ -41,7 +41,8 @@
      agg, dpre, dagg_0, dagg_1, dagg_2, dagg_3, dx, col_send, col_recv,
      codes_s, codes_r, part_s, part_r, dagg_s, dagg_r, col_s, col_r,
      codes_ref, book_ref, adj_ref, ws_ref, wn_ref, bias_ref, cot_ref, in_sems, table,
-     out_ref, gsn_ref, gb_ref, gc_ref, out_sems) = refs[13:54]
+     out_ref, gsn_ref, gb_ref, gc_ref, out_sems,
+     relay_own, relay_recv, relay_s, relay_r, hand_s) = refs[13:59]
     loads = [
         pltpu.make_async_copy(src, dst, in_sems.at[at])
         for at, (src, dst) in enumerate(
@@ -71,6 +72,17 @@
 
     def dom_source(k):
         return lax.rem(d + doms - k, doms)
+
+    line = doms == 4
+    inner = (d == 1) | (d == 2)
+    outer = jnp.logical_not(inner)
+    beside = jnp.where(d < 2, 1 - d, 5 - d)
+
+    def unless_far(k, fn, low_end, high_end):
+        if line and k in (low_end, high_end):
+            pl.when(d != (0 if k == low_end else 3))(fn)
+        else:
+            fn()
 
     def copy(src, dst, send, recv, device):
         return pltpu.make_async_remote_copy(
@@ -136,17 +148,45 @@
     def part_copy(c, k):
         return copy(part_send.at[c, k], part_recv.at[c, k], part_s.at[c, k], part_r.at[c, k], dom_peer(k)[1])
 
+    def relay_copy(c, slot):
+        return copy(part_send.at[c, slot], relay_recv.at[c], relay_s.at[c], relay_r.at[c], {"dom": beside})
+
     for c in range(CHUNKS):
         rows = slice(c * part, (c + 1) * part)
         prods = [mm(adj_ref[s, rows, :], slot_t[s], NT) * live[s] for s in range(slots)]
-        for k in list(range(1, doms)) + [0]:
+        for k in (3, 1, 2, 0) if line else list(range(1, doms)) + [0]:
             to = dom_peer(k)[0]
             total = sum(prods[s] * jnp.where(row_dom[s] == to, 1.0, 0.0).astype(F32) for s in range(slots))
-            if k:
+            if k == 0:
+                part_own[rows, :] = total
+            elif line and k == 2:
+                relay_own[c] = total
+
+                @pl.when(outer)
+                def _():
+                    part_send[c, 2] = relay_own[c].astype(BF16)
+                    part_copy(c, 2).start()
+            else:
                 part_send[c, k] = total.astype(BF16)
-                part_copy(c, k).start()
-            else:
-                part_own[rows, :] = total
+                if line:
+                    end = 0 if k == 3 else 3
+                    pl.when(d == end)(lambda: relay_copy(c, k).start())
+                    pl.when(d != end)(lambda: part_copy(c, k).start())
+                else:
+                    part_copy(c, k).start()
+
+    if line:
+        for c in range(CHUNKS):
+            @pl.when(inner)
+            def _():
+                relay_copy(c, 1).wait_recv()
+                part_send[c, 2] = (relay_own[c] + relay_recv[c].astype(F32)).astype(BF16)
+                part_copy(c, 2).start()
+
+            for k, end in ((1, 0), (3, 3)):
+                @pl.when(d == end)
+                def _():
+                    part_recv[c, k] = jnp.zeros((part, feat), BF16)
 
     cent_ids = lax.broadcasted_iota(jnp.int32, (cents, side), 0)
 
@@ -169,7 +209,7 @@
         rows = slice(c * part, (c + 1) * part)
         total = part_own[rows, :]
         for k in range(1, doms):
-            part_copy(c, k).wait_recv()
+            unless_far(k, lambda: part_copy(c, k).wait_recv(), 1, 3)
             total = total + part_recv[c, k].astype(F32)
         low = total.astype(BF16)
         agg[rows, :] = low
@@ -189,7 +229,7 @@
     for c in range(PARTS):
         dagg_all[c][d] = mm(wn_ref[c * fpart:(c + 1) * fpart, :], dpre_all, NT).astype(BF16)
         for k in range(1, doms):
-            dagg_copy(c, k).start()
+            unless_far(k, lambda: dagg_copy(c, k).start(), 3, 1)
     stores[0].start()
 
     grad_self = mm(feats_t[...], dpre_all)
@@ -199,7 +239,7 @@
     if reduce_here:
         (gs, g_recv, g_mid, g_fin, cs, c_recv, c_mid, c_fin, b_grp, b_dom,
          g1s, g1r, g2s, g2r, g4s, g4r, c1s, c1r, c2s, c2r, c4s, c4r,
-         b1s, b1r, b2s, b2r) = refs[54:]
+         b1s, b1r, b2s, b2r) = refs[59:]
 
         def rs_group(src, dst, ss, rr):
             def go(k):
@@ -263,10 +303,18 @@
     def col_copy(c, k):
         return copy(col_send.at[k, c], col_recv.at[k, c], col_s.at[c, k], col_r.at[c, k], group_peer(k)[1])
 
+    def hand_on(c):
+        at = dagg_all[c].at[dom_source(2)]
+        return copy(at, at, hand_s.at[c], dagg_r.at[c, 2 * d - 1], {"dom": beside})
+
     for c in range(PARTS):
         rows = slice(c * fpart, (c + 1) * fpart)
-        for k in range(1, doms):
-            dagg_wait(c, k)
+        if line:
+            dagg_wait(c, 2)
+            pl.when(inner)(lambda: hand_on(c).start())
+        for k in range(1, doms):
+            if not (line and k == 2):
+                dagg_wait(c, k)
         prods = [mm(dagg_all[c][row_dom[s]], adj_ref[s]) * live[s] for s in range(slots)]
 
         def column(k):
@@ -361,10 +409,14 @@
     for c in range(PARTS):
         each(1, group, functools.partial(lambda c, k: col_copy(c, k).wait_send(), c))
         for k in range(1, doms):
-            dagg_copy(c, k).wait_send()
+            unless_far(k, lambda: dagg_copy(c, k).wait_send(), 3, 1)
+        if line:
+            pl.when(inner)(lambda: hand_on(c).wait_send())
     for c in range(CHUNKS):
         for k in range(1, doms):
-            part_copy(c, k).wait_send()
+            unless_far(k, lambda: part_copy(c, k).wait_send(), 3, 1)
+        if line:
+            pl.when(outer)(lambda: relay_copy(c, 1).wait_send())
     for store in stores:
         store.wait()
 
@@ -406,6 +458,7 @@
         vm((subs, side), jnp.int32), vm((feat, cents), BF16), vm((slots, side, side), BF16), vm((feat, feat), BF16),
         vm((feat, feat), BF16), vm((1, feat), F32), vm((side, feat), BF16), dma((7,)), vm((feat, cents), F32),
         vm((side, feat), BF16), vm((2 * feat, feat), F32), vm((8, feat), F32), vm((feat, cents), F32), dma((4,)),
+        vm((CHUNKS, part, feat), F32), vm((CHUNKS, part, feat), BF16), dma((CHUNKS,)), dma((CHUNKS,)), dma((PARTS,)),
     ]
     if reduce_here:
         piece, lanes = 2 * feat // group, cents // 2

time: 63.7 us -> 61.2 us (0.961)
  Pallas kernels: 62.2 us -> 59.7 us
    pallas_call x1, Pallas kernels: 60.3 us -> 57.7 us  [body(): pl.pallas_call(functools.partial(kernel, cfg), out_shape=(jax.ShapeDtypeS...]
where the time goes in v4:
time: 61.2 us; the launch traced here: 61 us
  Pallas kernels  59.7 us (98%)
  between operations  1.29 us (2%)
    pallas_call x1, Pallas kernels, body(): pl.pallas_call(functools.partial(kernel, cfg), out_shape=(jax.ShapeDtypeS...  57.7 us
    pallas_call x1, Pallas kernels, body(): pl.pallas_call(write_out, out_shape=(jax.ShapeDtypeStruct((side, feat), B...  1.95 us

profile of v4, /device:TPU:0, one launch (start us, length us, event | category | flops | bytes accessed | tf_op | source)
XLA Modules:
  0.0 61.0 jit_solution(8905260308951978655)
XLA Ops:
  1.3 57.7 %shard_map.128 = (bf16[256,256]{1,0:T(8,128)(2,1)}, f32[512,256]{1,0:T(8,128)}, f32[8,256]{1,0:T(8,128)}, f32[256,256]{1,0:T(8,128)}) custom-call(s32[2,4]{1,0:T(2,128)} %bitcast.16, s32[1]{0:T(128)S(6)} %copy.14.refs_1_, s32[32,256]{1,0:T(8,128)} %bitcast.15, bf16[256,256]{1,0:T(8,128)(2,1)} %bitcast.14, bf16[4,256,256]{2,1,0:T(8,128)(2,1)} %bitcast.13, ...), custom_call_target="tpu_custom_call" | custom-call | tf_op jit(solution)/shard_map/pallas_call | solution.py:478
  59.0 2.0 %shard_map.129 = (bf16[256,256]{1,0:T(8,128)(2,1)}, f32[256,256]{1,0:T(8,128)}, f32[256,256]{1,0:T(8,128)}, f32[1,256]{1,0:T(1,128)}, f32[256,256]{1,0:T(8,128)}) custom-call(bf16[256,256]{1,0:T(8,128)(2,1)} %get-tuple-element.14.node_in, f32[512,256]{1,0:T(8,128)} %get-tuple-element.15.gsn_in, f32[8,256]{1,0:T(8,128)} %get-tuple-element.16.gb_in, ...), custom_call_target="tpu_custom_call" | custom-call | tf_op jit(solution)/shard_map/pallas_call | solution.py:503

commit v5 on v4

--- a/solution.py
+++ b/solution.py
@@ -42,7 +42,7 @@
      codes_s, codes_r, part_s, part_r, dagg_s, dagg_r, col_s, col_r,
      codes_ref, book_ref, adj_ref, ws_ref, wn_ref, bias_ref, cot_ref, in_sems, table,
      out_ref, gsn_ref, gb_ref, gc_ref, out_sems,
-     relay_own, relay_recv, relay_s, relay_r, hand_s) = refs[13:59]
+     relay_own, relay_recv, relay_s, relay_r, hand_s, pair_send, pair_recv, pair_own, pair_s, pair_r) = refs[13:64]
     loads = [
         pltpu.make_async_copy(src, dst, in_sems.at[at])
         for at, (src, dst) in enumerate(
@@ -239,7 +239,7 @@
     if reduce_here:
         (gs, g_recv, g_mid, g_fin, cs, c_recv, c_mid, c_fin, b_grp, b_dom,
          g1s, g1r, g2s, g2r, g4s, g4r, c1s, c1r, c2s, c2r, c4s, c4r,
-         b1s, b1r, b2s, b2r) = refs[59:]
+         b1s, b1r, b2s, b2r) = refs[64:]
 
         def rs_group(src, dst, ss, rr):
             def go(k):
@@ -301,32 +301,54 @@
     dx[...] = mm(ws_ref[...], dpre_all, NT)
 
     def col_copy(c, k):
-        return copy(col_send.at[k, c], col_recv.at[k, c], col_s.at[c, k], col_r.at[c, k], group_peer(k)[1])
+        device = group_peer(2 * k)[1]
+        return copy(col_send.at[k, c], col_recv.at[k, c], col_s.at[c, k], col_r.at[c, k], device)
+
+    beside_rep = g + 1 - 2 * lax.rem(g, 2)
+
+    def pair_copy(c):
+        device = {"tile": lax.div(beside_rep, reps), "rep": lax.rem(beside_rep, reps)}
+        return copy(pair_send.at[c], pair_recv.at[c], pair_s.at[c], pair_r.at[c], device)
+
+    def finish_part(c):
+        pair_copy(c).wait_recv()
+
+        def send_column(k):
+            col_send[k, c] = (pair_own[c, k] + pair_recv[c, k].astype(F32)).astype(BF16)
+            col_copy(c, k).start()
+
+        each(1, group // 2, send_column)
+        rows = slice(c * fpart, (c + 1) * fpart)
+        dx[rows, :] = dx[rows, :] + pair_own[c, 0] + pair_recv[c, 0].astype(F32)
 
     def hand_on(c):
         at = dagg_all[c].at[dom_source(2)]
         return copy(at, at, hand_s.at[c], dagg_r.at[c, 2 * d - 1], {"dom": beside})
 
     for c in range(PARTS):
-        rows = slice(c * fpart, (c + 1) * fpart)
         if line:
             dagg_wait(c, 2)
             pl.when(inner)(lambda: hand_on(c).start())
+        if c:
+            finish_part(c - 1)
         for k in range(1, doms):
             if not (line and k == 2):
                 dagg_wait(c, k)
         prods = [mm(dagg_all[c][row_dom[s]], adj_ref[s]) * live[s] for s in range(slots)]
 
-        def column(k):
-            to = group_peer(k)[0]
+        def column(to):
             return sum(prods[s] * jnp.where(col_pos[s] == to, 1.0, 0.0).astype(F32) for s in range(slots))
 
-        def send_column(k):
-            col_send[k, c] = column(k).astype(BF16)
-            col_copy(c, k).start()
-
-        each(1, group, send_column)
-        dx[rows, :] = dx[rows, :] + column(0)
+        def give(k):
+            pair_send[c, k] = column(lax.rem(beside_rep + 2 * k, group)).astype(BF16)
+
+        def keep(k):
+            pair_own[c, k] = column(lax.rem(g + 2 * k, group))
+
+        each(0, group // 2, give)
+        pair_copy(c).start()
+        each(0, group // 2, keep)
+    finish_part(PARTS - 1)
 
     if reduce_here:
         mid = gs[g].astype(F32)
@@ -348,7 +370,7 @@
             col_copy(c, k).wait_recv()
             dx[base:base + fpart, :] = dx[base:base + fpart, :] + col_recv[k, c].astype(F32)
 
-        each(1, group, add_column)
+        each(1, group // 2, add_column)
         for at in range(fpart // width):
             rows = slice(base + at * width, base + (at + 1) * width)
             full = dx[rows, :]
@@ -407,7 +429,8 @@
 
     each(1, group, lambda k: codes_copy(k).wait_send())
     for c in range(PARTS):
-        each(1, group, functools.partial(lambda c, k: col_copy(c, k).wait_send(), c))
+        each(1, group // 2, functools.partial(lambda c, k: col_copy(c, k).wait_send(), c))
+        pair_copy(c).wait_send()
         for k in range(1, doms):
             unless_far(k, lambda: dagg_copy(c, k).wait_send(), 3, 1)
         if line:
@@ -452,13 +475,15 @@
         vm((feat, side), BF16), vm((slots, feat, side), BF16), vm((side, feat), BF16), vm((side, feat), F32),
         vm((side, feat), F32), vm((CHUNKS, doms, part, feat), BF16), vm((CHUNKS, doms, part, feat), BF16),
         vm((side, feat), BF16), vm((side, feat), BF16), *[vm((doms, feat // PARTS, side), BF16)] * PARTS, vm((feat, side), F32),
-        vm((group, PARTS, feat // PARTS, side), BF16), vm((group, PARTS, feat // PARTS, side), BF16),
+        vm((group // 2, PARTS, feat // PARTS, side), BF16), vm((group // 2, PARTS, feat // PARTS, side), BF16),
         dma((group,)), dma((group,)), dma((CHUNKS, doms)), dma((CHUNKS, doms)),
-        dma((PARTS, doms)), dma((PARTS, doms)), dma((PARTS, group)), dma((PARTS, group)),
+        dma((PARTS, doms)), dma((PARTS, doms)), dma((PARTS, group // 2)), dma((PARTS, group // 2)),
         vm((subs, side), jnp.int32), vm((feat, cents), BF16), vm((slots, side, side), BF16), vm((feat, feat), BF16),
         vm((feat, feat), BF16), vm((1, feat), F32), vm((side, feat), BF16), dma((7,)), vm((feat, cents), F32),
         vm((side, feat), BF16), vm((2 * feat, feat), F32), vm((8, feat), F32), vm((feat, cents), F32), dma((4,)),
         vm((CHUNKS, part, feat), F32), vm((CHUNKS, part, feat), BF16), dma((CHUNKS,)), dma((CHUNKS,)), dma((PARTS,)),
+        vm((PARTS, group // 2, feat // PARTS, side), BF16), vm((PARTS, group // 2, feat // PARTS, side), BF16),
+        vm((PARTS, group // 2, feat // PARTS, side), F32), dma((PARTS,)), dma((PARTS,)),
     ]
     if reduce_here:
         piece, lanes = 2 * feat // group, cents // 2

time: 61.2 us -> 62.4 us (1.020)
  Pallas kernels: 59.7 us -> 61 us
    pallas_call x1, Pallas kernels: 57.7 us -> 59 us  [body(): pl.pallas_call(functools.partial(kernel, cfg), out_shape=(jax.ShapeDtypeS...]
where the time goes in v5:
time: 62.4 us; the launch traced here: 62.3 us
  Pallas kernels  61 us (98%)
  between operations  1.29 us (2%)
    pallas_call x1, Pallas kernels, body(): pl.pallas_call(functools.partial(kernel, cfg), out_shape=(jax.ShapeDtypeS...  59 us
    pallas_call x1, Pallas kernels, body(): pl.pallas_call(write_out, out_shape=(jax.ShapeDtypeStruct((side, feat), B...  1.95 us

profile of v5, /device:TPU:0, one launch (start us, length us, event | category | flops | bytes accessed | tf_op | source)
XLA Modules:
  0.0 62.3 jit_solution(4313384547971688302)
XLA Ops:
  1.3 59.0 %shard_map.128 = (bf16[256,256]{1,0:T(8,128)(2,1)}, f32[512,256]{1,0:T(8,128)}, f32[8,256]{1,0:T(8,128)}, f32[256,256]{1,0:T(8,128)}) custom-call(s32[2,4]{1,0:T(2,128)} %bitcast.16, s32[1]{0:T(128)S(6)} %copy.14.refs_1_, s32[32,256]{1,0:T(8,128)} %bitcast.15, bf16[256,256]{1,0:T(8,128)(2,1)} %bitcast.14, bf16[4,256,256]{2,1,0:T(8,128)(2,1)} %bitcast.13, ...), custom_call_target="tpu_custom_call" | custom-call | tf_op jit(solution)/shard_map/pallas_call | solution.py:503
  60.3 2.0 %shard_map.129 = (bf16[256,256]{1,0:T(8,128)(2,1)}, f32[256,256]{1,0:T(8,128)}, f32[256,256]{1,0:T(8,128)}, f32[1,256]{1,0:T(1,128)}, f32[256,256]{1,0:T(8,128)}) custom-call(bf16[256,256]{1,0:T(8,128)(2,1)} %get-tuple-element.14.node_in, f32[512,256]{1,0:T(8,128)} %get-tuple-element.15.gsn_in, f32[8,256]{1,0:T(8,128)} %get-tuple-element.16.gb_in, ...), custom_call_target="tpu_custom_call" | custom-call | tf_op jit(solution)/shard_map/pallas_call | solution.py:528

commit v6 on v4

--- a/solution.py
+++ b/solution.py
@@ -13,6 +13,7 @@
 NT = (((1,), (1,)), ((), ()))
 CHUNKS = 2
 PARTS = 4
+BATCH = 2
 LANES = 128
 ROWS16 = 16
 
@@ -307,6 +308,50 @@
         at = dagg_all[c].at[dom_source(2)]
         return copy(at, at, hand_s.at[c], dagg_r.at[c, 2 * d - 1], {"dom": beside})
 
+    lanes = cents // 2
+
+    def code_part(c):
+        base = c * fpart
+
+        def add_column(k):
+            col_copy(c, k).wait_recv()
+            dx[base:base + fpart, :] = dx[base:base + fpart, :] + col_recv[k, c].astype(F32)
+
+        each(1, group, add_column)
+        for at in range(fpart // width):
+            rows = slice(base + at * width, base + (at + 1) * width)
+            full = dx[rows, :]
+            high = full.astype(BF16).astype(F32)
+            both = jnp.concatenate([high, full - high], axis=0).astype(BF16)
+            two = mm(both, onehot[c * (fpart // width) + at], NT)
+            gc_ref[rows, :] = two[0:width, :] + two[width:2 * width, :]
+        if reduce_here:
+            for h in range(2):
+                cs[c // BATCH, h * half:(h + 1) * half, c % BATCH] = (
+                    gc_ref[base:base + fpart, h * lanes:(h + 1) * lanes].astype(BF16).reshape(half, fpart // half, lanes)
+                )
+            if c % BATCH == BATCH - 1:
+                for k in range(1, group):
+                    code_copy(c // BATCH, k).start()
+
+    def wait_sends_columns():
+        for c in range(PARTS):
+            each(1, group, functools.partial(lambda c, k: col_copy(c, k).wait_send(), c))
+
+    def wait_sends_dagg():
+        for c in range(PARTS):
+            for k in range(1, doms):
+                unless_far(k, lambda: dagg_copy(c, k).wait_send(), 3, 1)
+            if line:
+                pl.when(inner)(lambda: hand_on(c).wait_send())
+
+    each(1, group, lambda k: codes_copy(k).wait_send())
+    for c in range(CHUNKS):
+        for k in range(1, doms):
+            unless_far(k, lambda: part_copy(c, k).wait_send(), 3, 1)
+        if line:
+            pl.when(outer)(lambda: relay_copy(c, 1).wait_send())
+
     for c in range(PARTS):
         rows = slice(c * fpart, (c + 1) * fpart)
         if line:
@@ -327,6 +372,8 @@
 
         each(1, group, send_column)
         dx[rows, :] = dx[rows, :] + column(0)
+        if 2 <= c:
+            code_part(c - 2)
 
     if reduce_here:
         mid = gs[g].astype(F32)
@@ -340,42 +387,22 @@
         b_dom[d] = jnp.sum(b_grp[...], axis=0)
         start(b2[0], doms)
 
-    lanes = cents // 2
-    for c in range(PARTS):
-        base = c * fpart
-
-        def add_column(k):
-            col_copy(c, k).wait_recv()
-            dx[base:base + fpart, :] = dx[base:base + fpart, :] + col_recv[k, c].astype(F32)
-
-        each(1, group, add_column)
-        for at in range(fpart // width):
-            rows = slice(base + at * width, base + (at + 1) * width)
-            full = dx[rows, :]
-            high = full.astype(BF16).astype(F32)
-            both = jnp.concatenate([high, full - high], axis=0).astype(BF16)
-            two = mm(both, onehot[c * (fpart // width) + at], NT)
-            gc_ref[rows, :] = two[0:width, :] + two[width:2 * width, :]
-        if reduce_here:
-            for h in range(2):
-                cs[c, h * half:(h + 1) * half] = (
-                    gc_ref[base:base + fpart, h * lanes:(h + 1) * lanes].astype(BF16).reshape(half, fpart // half, lanes)
-                )
+    code_part(PARTS - 2)
+    if reduce_here:
+        for k in range(1, doms):
+            g2[1](k)
+        g_fin[g] = jnp.sum(g_mid[...].astype(F32), axis=0).astype(BF16)
+        start(g4[0], group)
+    code_part(PARTS - 1)
+    wait_sends_dagg()
+
+    if reduce_here:
+        for b in range(PARTS // BATCH):
+            mid = cs[b, g].astype(F32)
             for k in range(1, group):
-                code_copy(c, k).start()
-            if c == 1:
-                for k in range(1, doms):
-                    g2[1](k)
-                g_fin[g] = jnp.sum(g_mid[...].astype(F32), axis=0).astype(BF16)
-                start(g4[0], group)
-
-    if reduce_here:
-        for c in range(PARTS):
-            mid = cs[c, g].astype(F32)
-            for k in range(1, group):
-                code_copy(c, k).wait_recv()
-                mid = mid + c_recv[c, k].astype(F32)
-            c_mid[d, c] = mid.astype(BF16)
+                code_copy(b, k).wait_recv()
+                mid = mid + c_recv[b, k].astype(F32)
+            c_mid[d, b * BATCH:(b + 1) * BATCH] = mid.astype(BF16)
         start(c2[0], doms)
         for k in range(1, group):
             g4[1](k)
@@ -389,6 +416,13 @@
             c2[1](k)
         c_fin[g] = jnp.sum(c_mid[...].astype(F32), axis=0).astype(BF16)
         start(c4[0], group)
+        for go, n in sends[:-1]:
+            for k in range(1, n):
+                go(k).wait_send()
+        for b in range(PARTS // BATCH):
+            for k in range(1, group):
+                code_copy(b, k).wait_send()
+        wait_sends_columns()
         for k in range(1, group):
             c4[1](k)
         for h in range(2):
@@ -396,27 +430,13 @@
                 gc_ref[c * fpart:(c + 1) * fpart, h * lanes:(h + 1) * lanes] = (
                     c_fin[h * half:(h + 1) * half, c].astype(F32).reshape(fpart, lanes)
                 )
+    else:
+        wait_sends_columns()
     stores[3].start()
     if reduce_here:
-        for go, n in sends:
+        for go, n in sends[-1:]:
             for k in range(1, n):
                 go(k).wait_send()
-        for c in range(PARTS):
-            for k in range(1, group):
-                code_copy(c, k).wait_send()
-
-    each(1, group, lambda k: codes_copy(k).wait_send())
-    for c in range(PARTS):
-        each(1, group, functools.partial(lambda c, k: col_copy(c, k).wait_send(), c))
-        for k in range(1, doms):
-            unless_far(k, lambda: dagg_copy(c, k).wait_send(), 3, 1)
-        if line:
-            pl.when(inner)(lambda: hand_on(c).wait_send())
-    for c in range(CHUNKS):
-        for k in range(1, doms):
-            unless_far(k, lambda: part_copy(c, k).wait_send(), 3, 1)
-        if line:
-            pl.when(outer)(lambda: relay_copy(c, 1).wait_send())
     for store in stores:
         store.wait()
 
@@ -466,11 +486,11 @@
         scratch += [
             vm((group, piece, feat), BF16), vm((group, piece, feat), BF16),
             vm((doms, piece, feat), BF16), vm((group, piece, feat), BF16),
-            vm((PARTS, group, some, lanes), BF16), vm((PARTS, group, some, lanes), BF16),
+            vm((PARTS // BATCH, group, BATCH, some, lanes), BF16), vm((PARTS // BATCH, group, BATCH, some, lanes), BF16),
             vm((doms, PARTS, some, lanes), BF16), vm((group, PARTS, some, lanes), BF16),
         ]
         scratch += [vm((group, 8, feat), F32), vm((doms, 8, feat), F32)]
-        for first in ((group,), (PARTS, group)):
+        for first in ((group,), (PARTS // BATCH, group)):
             scratch += [dma(first)] * 2 + [dma((doms,))] * 2 + [dma((group,))] * 2
         scratch += [dma((group,))] * 2 + [dma((doms,))] * 2
     in_smem = pl.BlockSpec(memory_space=pltpu.SMEM)

time: 61.2 us -> 63.6 us (1.039)
  Pallas kernels: 59.7 us -> 62.1 us
    pallas_call x1, Pallas kernels: 57.7 us -> 60.2 us  [body(): pl.pallas_call(functools.partial(kernel, cfg), out_shape=(jax.ShapeDtypeS...]
where the time goes in v6:
time: 63.6 us; the launch traced here: 63.4 us
  Pallas kernels  62.1 us (98%)
  between operations  1.29 us (2%)
    pallas_call x1, Pallas kernels, body(): pl.pallas_call(functools.partial(kernel, cfg), out_shape=(jax.ShapeDtypeS...  60.2 us
    pallas_call x1, Pallas kernels, body(): pl.pallas_call(write_out, out_shape=(jax.ShapeDtypeStruct((side, feat), B...  1.95 us

profile of v6, /device:TPU:0, one launch (start us, length us, event | category | flops | bytes accessed | tf_op | source)
XLA Modules:
  0.0 63.4 jit_solution(3885023919850651349)
XLA Ops:
  1.3 60.2 %shard_map.128 = (bf16[256,256]{1,0:T(8,128)(2,1)}, f32[512,256]{1,0:T(8,128)}, f32[8,256]{1,0:T(8,128)}, f32[256,256]{1,0:T(8,128)}) custom-call(s32[2,4]{1,0:T(2,128)} %bitcast.16, s32[1]{0:T(128)S(6)} %copy.14.refs_1_, s32[32,256]{1,0:T(8,128)} %bitcast.15, bf16[256,256]{1,0:T(8,128)(2,1)} %bitcast.14, bf16[4,256,256]{2,1,0:T(8,128)(2,1)} %bitcast.13, ...), custom_call_target="tpu_custom_call" | custom-call | tf_op jit(solution)/shard_map/pallas_call | solution.py:498
  61.5 2.0 %shard_map.129 = (bf16[256,256]{1,0:T(8,128)(2,1)}, f32[256,256]{1,0:T(8,128)}, f32[256,256]{1,0:T(8,128)}, f32[1,256]{1,0:T(1,128)}, f32[256,256]{1,0:T(8,128)}) custom-call(bf16[256,256]{1,0:T(8,128)(2,1)} %get-tuple-element.14.node_in, f32[512,256]{1,0:T(8,128)} %get-tuple-element.15.gsn_in, f32[8,256]{1,0:T(8,128)} %get-tuple-element.16.gb_in, ...), custom_call_target="tpu_custom_call" | custom-call | tf_op jit(solution)/shard_map/pallas_call | solution.py:523

commit v7 on v4

--- a/solution.py
+++ b/solution.py
@@ -144,6 +144,7 @@
     for s in range(slots):
         codes_one[...] = codes_all[col_pos[s]].astype(F32).astype(jnp.int32)
         decode(codes_one, slot_t.at[s])
+        slot_t[s] = slot_t[s].astype(F32).T.astype(BF16)
 
     def part_copy(c, k):
         return copy(part_send.at[c, k], part_recv.at[c, k], part_s.at[c, k], part_r.at[c, k], dom_peer(k)[1])
@@ -153,7 +154,7 @@
 
     for c in range(CHUNKS):
         rows = slice(c * part, (c + 1) * part)
-        prods = [mm(adj_ref[s, rows, :], slot_t[s], NT) * live[s] for s in range(slots)]
+        prods = [mm(adj_ref[s, rows, :], slot_t[s]) * live[s] for s in range(slots)]
         for k in (3, 1, 2, 0) if line else list(range(1, doms)) + [0]:
             to = dom_peer(k)[0]
             total = sum(prods[s] * jnp.where(row_dom[s] == to, 1.0, 0.0).astype(F32) for s in range(slots))
@@ -188,15 +189,10 @@
                 def _():
                     part_recv[c, k] = jnp.zeros((part, feat), BF16)
 
-    cent_ids = lax.broadcasted_iota(jnp.int32, (cents, side), 0)
-
-    def hot_step(it, carry):
-        slab = codes_ref[pl.ds(pl.multiple_of(it * 8, 8), 8), :]
-        for at in range(8):
-            onehot[it * 8 + at] = jnp.where(slab[at:at + 1, :] == cent_ids, 1.0, 0.0).astype(BF16)
-        return carry
-
-    lax.fori_loop(0, subs // 8, hot_step, 0)
+    cent_ids = lax.broadcasted_iota(jnp.int32, (side, cents), 1).astype(F32)
+    by_node = codes_ref[...].astype(F32).T
+    for m in range(subs):
+        onehot[m] = jnp.where(by_node[:, m:m + 1] == cent_ids, 1.0, 0.0).astype(BF16)
 
     def dagg_copy(c, k):
         return copy(dagg_all[c].at[d], dagg_all[c].at[d], dagg_s.at[c, k], dagg_r.at[c, k], dom_peer(k)[1])
@@ -226,8 +222,9 @@
 
     dpre_all = dpre[...]
     fpart = feat // PARTS
+    dpre_t = dpre_all.astype(F32).T.astype(BF16)
     for c in range(PARTS):
-        dagg_all[c][d] = mm(wn_ref[c * fpart:(c + 1) * fpart, :], dpre_all, NT).astype(BF16)
+        dagg_all[c][d] = mm(wn_ref[c * fpart:(c + 1) * fpart, :], dpre_t).astype(BF16)
         for k in range(1, doms):
             unless_far(k, lambda: dagg_copy(c, k).start(), 3, 1)
     stores[0].start()
@@ -298,7 +295,7 @@
         stores[1].start()
         stores[2].start()
 
-    dx[...] = mm(ws_ref[...], dpre_all, NT)
+    dx[...] = mm(ws_ref[...], dpre_t)
 
     def col_copy(c, k):
         return copy(col_send.at[k, c], col_recv.at[k, c], col_s.at[c, k], col_r.at[c, k], group_peer(k)[1])
@@ -354,7 +351,7 @@
             full = dx[rows, :]
             high = full.astype(BF16).astype(F32)
             both = jnp.concatenate([high, full - high], axis=0).astype(BF16)
-            two = mm(both, onehot[c * (fpart // width) + at], NT)
+            two = mm(both, onehot[c * (fpart // width) + at])
             gc_ref[rows, :] = two[0:width, :] + two[width:2 * width, :]
         if reduce_here:
             for h in range(2):
@@ -448,7 +445,7 @@
     cfg = (doms, tiles, reps, slots, side, feat, subs, cents, reduce_here)
     vm, dma = pltpu.VMEM, pltpu.SemaphoreType.DMA
     scratch = [
-        vm((group, subs, side), BF16), vm((subs, side), jnp.int32), vm((subs, cents, side), BF16),
+        vm((group, subs, side), BF16), vm((subs, side), jnp.int32), vm((subs, side, cents), BF16),
         vm((feat, side), BF16), vm((slots, feat, side), BF16), vm((side, feat), BF16), vm((side, feat), F32),
         vm((side, feat), F32), vm((CHUNKS, doms, part, feat), BF16), vm((CHUNKS, doms, part, feat), BF16),
         vm((side, feat), BF16), vm((side, feat), BF16), *[vm((doms, feat // PARTS, side), BF16)] * PARTS, vm((feat, side), F32),

time: 61.2 us -> 61.6 us (level)
  no operation moved by 1% of the time
where the time goes in v7:
time: 61.6 us; the launch traced here: 61.4 us
  Pallas kernels  60.1 us (98%)
  between operations  1.29 us (2%)
    pallas_call x1, Pallas kernels, body(): pl.pallas_call(functools.partial(kernel, cfg), out_shape=(jax.ShapeDtypeS...  58.1 us
    pallas_call x1, Pallas kernels, body(): pl.pallas_call(write_out, out_shape=(jax.ShapeDtypeStruct((side, feat), B...  1.95 us

profile of v7, /device:TPU:0, one launch (start us, length us, event | category | flops | bytes accessed | tf_op | source)
XLA Modules:
  0.0 61.4 jit_solution(840971562100243058)
XLA Ops:
  1.3 58.1 %shard_map.128 = (bf16[256,256]{1,0:T(8,128)(2,1)}, f32[512,256]{1,0:T(8,128)}, f32[8,256]{1,0:T(8,128)}, f32[256,256]{1,0:T(8,128)}) custom-call(s32[2,4]{1,0:T(2,128)} %bitcast.16, s32[1]{0:T(128)S(6)} %copy.14.refs_1_, s32[32,256]{1,0:T(8,128)} %bitcast.15, bf16[256,256]{1,0:T(8,128)(2,1)} %bitcast.14, bf16[4,256,256]{2,1,0:T(8,128)(2,1)} %bitcast.13, ...), custom_call_target="tpu_custom_call" | custom-call | tf_op jit(solution)/shard_map/pallas_call | solution.py:475
  59.4 2.0 %shard_map.129 = (bf16[256,256]{1,0:T(8,128)(2,1)}, f32[256,256]{1,0:T(8,128)}, f32[256,256]{1,0:T(8,128)}, f32[1,256]{1,0:T(1,128)}, f32[256,256]{1,0:T(8,128)}) custom-call(bf16[256,256]{1,0:T(8,128)(2,1)} %get-tuple-element.14.node_in, f32[512,256]{1,0:T(8,128)} %get-tuple-element.15.gsn_in, f32[8,256]{1,0:T(8,128)} %get-tuple-element.16.gb_in, ...), custom_call_target="tpu_custom_call" | custom-call | tf_op jit(solution)/shard_map/pallas_call | solution.py:500
